TPU v7x, 32 devices: a whole 2x2x4 slice. The times are simulated.
32 devices in a mesh: wide: 8 (over z, y), narrow: 4 (over x, core).
Axes of the slice: x: 2, y: 2, z: 4, core: 2. Of those that a mesh axis runs over, the one named last changes fastest.
Arguments:
- tokens: bfloat16 [32768, 768], P(('wide', 'narrow')), may hold values from -6 to 6
- cotangent: bfloat16 [32768, 768], P(('wide', 'narrow')), may hold values from -6 to 6
- w_attn_in: bfloat16 [768, 2304], P(('wide', 'narrow')), may hold values from -0.21875 to 0.21875
- w_attn_out: bfloat16 [768, 768], P(('wide', 'narrow')), may hold values from -0.21875 to 0.21875
- w_fc_in: bfloat16 [768, 3072], P(('wide', 'narrow')), may hold values from -0.21875 to 0.21875
- w_fc_out: bfloat16 [3072, 768], P(('wide', 'narrow')), may hold values from -0.109375 to 0.109375
- gains_d: bfloat16 [3, 768], P(None, ('wide', 'narrow')), may hold values from 0.099609375 to 1.8984375
- biases_d: bfloat16 [7, 768], P(None, ('wide', 'narrow')), may hold values from -3 to 3
- gains_ff: bfloat16 [3072], P(('wide', 'narrow')), may hold values from 0.099609375 to 1.8984375
- biases_ff: bfloat16 [2, 3072], P(None, ('wide', 'narrow')), may hold values from -3 to 3
- rel_table: bfloat16 [12, 1024], P(None, ('wide', 'narrow')), may hold values from -4 to 4
- head_scale: bfloat16 [12], replicated, may hold values from 0.5 to 2
- bucket: int32 [512], P(('wide', 'narrow')), may hold values from 0 to 2, as said below
- lengths: int32 [512], P(('wide', 'narrow')), may hold values from 0 to 225, as said below
Outputs:
- out_tokens: bfloat16 [32768, 768], P(('wide', 'narrow'))
- grad_tokens: bfloat16 [32768, 768], P(('wide', 'narrow'))
- grad_attn_in: float32 [768, 2304], P(('wide', 'narrow'))
- grad_attn_out: float32 [768, 768], P(('wide', 'narrow'))
- grad_fc_in: float32 [768, 3072], P(('wide', 'narrow'))
- grad_fc_out: float32 [3072, 768], P(('wide', 'narrow'))
- grad_gains_d: float32 [3, 768], P(None, ('wide', 'narrow'))
- grad_biases_d: float32 [7, 768], P(None, ('wide', 'narrow'))
- grad_gains_ff: float32 [3072], P(('wide', 'narrow'))
- grad_biases_ff: float32 [2, 3072], P(None, ('wide', 'narrow'))
- grad_rel_table: float32 [12, 1024], P(None, ('wide', 'narrow'))
- grad_head_scale: float32 [12], replicated
Inputs may be any that keep to these rules, and one draw needn't show every extreme that they name: On each device's 16 slots in order: between 1 and 3 images of bucket 1 (a 15 x 15 patch grid in 256 token places), then images of bucket 0 (a 8 x 8 grid in 64 places) that fill the device's 1024 places exactly, then empty slots with id 2. `lengths`: live tokens of each image, in row-major patch order from its first place: at least half of its grid and at most all of it; 0 for empty slots. Each device's first bucket 1 image and first bucket 0 image are whole.
All inputs are finite; a program needn't handle non-finite values.
Results may differ from a plain program's by a relative error of at most 0.013.
Values may be sent and summed in bfloat16 or wider, within the bound.
No kernel may reach another device: no remote copies, remote signals or barrier semaphores. Data moves between devices by JAX's collectives and lax.ppermute only.
A program may use at most 256 MiB of HBM per device.

v0:
```python
import jax
import jax.numpy as jnp
from jax import lax
from jax.sharding import PartitionSpec as P

HEADS = 12
HEAD_DIM = 64
D = 768
GRID_L = 15
GRID_S = 8
SLOT_L = 256
SLOT_S = 64
BLOCK = 512
STRIDE = 32
RELS = 1024


PRECISE = lax.Precision.HIGHEST
NEG_FILL = -1e30
NORM_EPS = 1e-05
HALF_ROOT = 0.7071067811865476
DENSITY_SCALE = 0.3989422804014327
QUERY_SCALE = 0.125


def token_layout(bucket, lengths, row_count):
    slot_size = jnp.where(bucket == 1, SLOT_L, jnp.where(bucket == 0, SLOT_S, 0)).astype(jnp.int32)
    slot_end = jnp.cumsum(slot_size, dtype=jnp.int32)
    slot_start = slot_end - slot_size
    places = jnp.arange(row_count, dtype=jnp.int32)
    picture = jnp.sum(
        (slot_end[None, :] <= places[:, None]).astype(jnp.int32), axis=1, dtype=jnp.int32
    )
    picked = picture[:, None] == jnp.arange(bucket.shape[0], dtype=jnp.int32)[None, :]
    first_place = jnp.sum(jnp.where(picked, slot_start[None, :], 0), axis=1, dtype=jnp.int32)
    live_count = jnp.sum(jnp.where(picked, lengths[None, :], 0), axis=1, dtype=jnp.int32)
    slot_kind = jnp.sum(jnp.where(picked, bucket[None, :], 0), axis=1, dtype=jnp.int32)
    offset = places - first_place
    grid_width = jnp.where(slot_kind == 1, GRID_L, GRID_S).astype(jnp.int32)
    row_at = jnp.minimum(offset // grid_width, GRID_L - 1)
    col_at = offset % grid_width
    return (picture, row_at, col_at, offset < live_count)


def normalize(values, scale_by, shift_by):
    center = values - jnp.mean(values, axis=-1, keepdims=True)
    spread = lax.rsqrt(jnp.mean(center * center, axis=-1, keepdims=True) + NORM_EPS)
    scaled = center * spread
    return (scaled * scale_by + shift_by, scaled, spread)


def normalize_back(grad_out, scale_by, scaled, spread):
    inner_grad = grad_out * scale_by
    return spread * (
        inner_grad
        - jnp.mean(inner_grad, axis=-1, keepdims=True)
        - scaled * jnp.mean(inner_grad * scaled, axis=-1, keepdims=True)
    )


def rows_product(left_side, right_side):
    return lax.dot_general(
        left_side, right_side, (((0,), (0,)), ((), ())), preferred_element_type=jnp.float32
    )


def cols_product(left_side, right_side):
    return lax.dot_general(
        left_side, right_side, (((1,), (1,)), ((), ())), preferred_element_type=jnp.float32
    )


def pair_bias(bias_table):
    position = jnp.arange(GRID_L * GRID_L, dtype=jnp.int32)
    pos_row = position // GRID_L
    pos_col = position % GRID_L
    pair_index = (pos_row[:, None] - pos_row[None, :] + GRID_L) * STRIDE + (
        pos_col[:, None] - pos_col[None, :] + GRID_L
    )
    return jnp.take(bias_table, pair_index, axis=1)


def offset_table():
    grid_pos = jnp.arange(GRID_L, dtype=jnp.int32)
    difference = grid_pos[:, None] - grid_pos[None, :] + GRID_L
    return (difference[:, :, None] == jnp.arange(STRIDE, dtype=jnp.int32)[None, None, :]).astype(
        jnp.float32
    )


def block_scores(query_block, key_block, pair_table, pic_block, row_block, col_block, live_block):
    usable = (pic_block[:, None] == pic_block[None, :]) & live_block[None, :]
    position = row_block * GRID_L + col_block
    place_onehot = (
        position[:, None] == jnp.arange(GRID_L * GRID_L, dtype=jnp.int32)[None, :]
    ).astype(jnp.float32)
    left_bias = jnp.einsum(
        "qp,hpr->hqr",
        place_onehot,
        pair_table,
        precision=PRECISE,
        preferred_element_type=jnp.float32,
    )
    bias_part = jnp.einsum(
        "hqr,kr->hqk",
        left_bias,
        place_onehot,
        precision=PRECISE,
        preferred_element_type=jnp.float32,
    )
    scores = jnp.einsum("qhd,khd->hqk", query_block, key_block, preferred_element_type=jnp.float32)
    return (jnp.where(usable[None], scores + bias_part, NEG_FILL), place_onehot)


def attend(pair_table):

    def attend_block(pieces):
        query_block, key_block, value_block, pic_block, row_block, col_block, live_block = pieces
        scores, place_onehot = block_scores(
            query_block, key_block, pair_table, pic_block, row_block, col_block, live_block
        )
        largest = jnp.max(scores, axis=-1, keepdims=True)
        exponent = jnp.exp(scores - largest)
        row_total = jnp.sum(exponent, axis=-1, keepdims=True)
        attn_probs = (exponent / row_total).astype(jnp.bfloat16)
        attn_mixed = jnp.einsum(
            "hqk,khd->qhd", attn_probs, value_block, preferred_element_type=jnp.float32
        )
        return (attn_mixed, largest[..., 0] + jnp.log(row_total[..., 0]))

    return attend_block


def attend_back(pair_table, shifts):

    def back_block(pieces):
        (
            query_block,
            key_block,
            value_block,
            grad_block,
            log_total,
            pic_block,
            row_block,
            col_block,
            live_block,
        ) = pieces
        scores, place_onehot = block_scores(
            query_block, key_block, pair_table, pic_block, row_block, col_block, live_block
        )
        attn_probs = jnp.exp(scores - log_total[..., None])
        grad_probs = jnp.einsum(
            "qhd,khd->hqk", grad_block, value_block, preferred_element_type=jnp.float32
        )
        grad_value = jnp.einsum(
            "hqk,qhd->khd",
            attn_probs.astype(jnp.bfloat16),
            grad_block,
            preferred_element_type=jnp.float32,
        )
        centre = jnp.sum(attn_probs * grad_probs, axis=-1, keepdims=True)
        grad_scores = (attn_probs * (grad_probs - centre)).astype(jnp.bfloat16)
        grad_query = jnp.einsum(
            "hqk,khd->qhd", grad_scores, key_block, preferred_element_type=jnp.float32
        )
        grad_key = jnp.einsum(
            "hqk,qhd->khd", grad_scores, query_block, preferred_element_type=jnp.float32
        )
        by_key = jnp.einsum(
            "hqk,kp->hqp",
            grad_scores,
            place_onehot.astype(jnp.bfloat16),
            preferred_element_type=jnp.float32,
        )
        by_pair = jnp.einsum(
            "qr,hqp->hrp",
            place_onehot,
            by_key,
            precision=PRECISE,
            preferred_element_type=jnp.float32,
        )
        by_pair = by_pair.reshape(HEADS, GRID_L, GRID_L, GRID_L, GRID_L)
        by_rowoff = jnp.einsum(
            "hrcsd,rsa->hacd",
            by_pair,
            shifts,
            precision=PRECISE,
            preferred_element_type=jnp.float32,
        )
        grad_table = jnp.einsum(
            "hacd,cdb->hab",
            by_rowoff,
            shifts,
            precision=PRECISE,
            preferred_element_type=jnp.float32,
        ).reshape(HEADS, RELS)
        return (
            grad_query.astype(jnp.bfloat16),
            grad_key.astype(jnp.bfloat16),
            grad_value.astype(jnp.bfloat16),
            grad_table,
        )

    return back_block


def body(
    tokens,
    cotangent,
    w_attn_in,
    w_attn_out,
    w_fc_in,
    w_fc_out,
    gains_d,
    biases_d,
    gains_ff,
    biases_ff,
    rel_table,
    head_scale,
    bucket,
    lengths,
):
    gathered = (
        lax.all_gather(w_attn_in, ("wide", "narrow"), axis=0, tiled=True),
        lax.all_gather(w_attn_out, ("wide", "narrow"), axis=0, tiled=True),
        lax.all_gather(w_fc_in, ("wide", "narrow"), axis=0, tiled=True),
        lax.all_gather(w_fc_out, ("wide", "narrow"), axis=0, tiled=True),
        lax.all_gather(gains_d, ("wide", "narrow"), axis=1, tiled=True),
        lax.all_gather(biases_d, ("wide", "narrow"), axis=1, tiled=True),
        lax.all_gather(gains_ff, ("wide", "narrow"), axis=0, tiled=True),
        lax.all_gather(biases_ff, ("wide", "narrow"), axis=1, tiled=True),
        lax.all_gather(rel_table, ("wide", "narrow"), axis=1, tiled=True),
    )
    attn_in, attn_out, fc_in, fc_out, gain_rows, bias_rows, gain_mid, bias_mid, table_rows = (
        gathered
    )
    gain_rows = gain_rows.astype(jnp.float32)
    bias_rows = bias_rows.astype(jnp.float32)
    gain_mid = gain_mid.astype(jnp.float32)
    bias_mid = bias_mid.astype(jnp.float32)
    bias_table = table_rows.astype(jnp.float32)
    head_wide = jnp.repeat(head_scale.astype(jnp.float32), HEAD_DIM)
    row_count = tokens.shape[0]
    block_count = row_count // BLOCK
    picture, row_at, col_at, live_mask = token_layout(bucket, lengths, row_count)
    live_rows = live_mask.astype(jnp.float32)[:, None]
    inputs = tokens.astype(jnp.float32)
    normed_in, scaled_in, spread_in = normalize(inputs, gain_rows[0], bias_rows[0])
    hidden_in = normed_in.astype(jnp.bfloat16)
    projected = jnp.dot(hidden_in, attn_in, preferred_element_type=jnp.float32)
    queries = ((projected[:, :D] + bias_rows[1]) * QUERY_SCALE).astype(jnp.bfloat16)
    key_rows = projected[:, D : 2 * D].astype(jnp.bfloat16)
    value_rows = (projected[:, 2 * D :] + bias_rows[2]).astype(jnp.bfloat16)
    head_shape = (block_count, BLOCK, HEADS, HEAD_DIM)
    query_blocks = queries.reshape(head_shape)
    key_blocks = key_rows.reshape(head_shape)
    value_blocks = value_rows.reshape(head_shape)
    geometry = (
        picture.reshape(block_count, BLOCK),
        row_at.reshape(block_count, BLOCK),
        col_at.reshape(block_count, BLOCK),
        live_mask.reshape(block_count, BLOCK),
    )
    attn_mixed, log_total = lax.map(
        attend(pair_bias(bias_table)), (query_blocks, key_blocks, value_blocks) + geometry
    )
    attn_mixed = attn_mixed.reshape(row_count, D)
    normed_attn, scaled_attn, spread_attn = normalize(
        attn_mixed * head_wide, gain_rows[1], bias_rows[3]
    )
    attn_low = normed_attn.astype(jnp.bfloat16)
    residual_mid = (
        inputs + jnp.dot(attn_low, attn_out, preferred_element_type=jnp.float32) + bias_rows[4]
    )
    normed_mid, scaled_mid, spread_mid = normalize(residual_mid, gain_rows[2], bias_rows[5])
    hidden_mid = normed_mid.astype(jnp.bfloat16)
    pre_act = jnp.dot(hidden_mid, fc_in, preferred_element_type=jnp.float32) + bias_mid[0]
    cumulative = 0.5 * (1.0 + lax.erf(pre_act * HALF_ROOT))
    normed_ff, scaled_ff, spread_ff = normalize(pre_act * cumulative, gain_mid, bias_mid[1])
    hidden_ff = normed_ff.astype(jnp.bfloat16)
    output_rows = (
        residual_mid + jnp.dot(hidden_ff, fc_out, preferred_element_type=jnp.float32) + bias_rows[6]
    )
    out_tokens = (output_rows * live_rows).astype(jnp.bfloat16)
    regathered = (
        lax.all_gather(w_attn_in, ("wide", "narrow"), axis=0, tiled=True),
        lax.all_gather(w_attn_out, ("wide", "narrow"), axis=0, tiled=True),
        lax.all_gather(w_fc_in, ("wide", "narrow"), axis=0, tiled=True),
        lax.all_gather(w_fc_out, ("wide", "narrow"), axis=0, tiled=True),
        lax.all_gather(gains_d, ("wide", "narrow"), axis=1, tiled=True),
        lax.all_gather(gains_ff, ("wide", "narrow"), axis=0, tiled=True),
        lax.all_gather(rel_table, ("wide", "narrow"), axis=1, tiled=True),
    )
    back_in, back_out, back_fc_in, back_fc_out = (
        regathered[0],
        regathered[1],
        regathered[2],
        regathered[3],
    )
    gain_back = regathered[4].astype(jnp.float32)
    gain_mid_back = regathered[5].astype(jnp.float32)
    table_back = regathered[6].astype(jnp.float32)
    grad_rows = cotangent.astype(jnp.float32) * live_rows
    grad_out_low = grad_rows.astype(jnp.bfloat16)
    grad_fc_out = rows_product(hidden_ff, grad_out_low)
    grad_bias_out = jnp.sum(grad_out_low.astype(jnp.float32), axis=0)
    grad_ff = cols_product(grad_out_low, back_fc_out)
    grad_gain_mid = jnp.sum(grad_ff * scaled_ff, axis=0)
    grad_bias_mid = jnp.sum(grad_ff, axis=0)
    grad_act = normalize_back(grad_ff, gain_mid_back, scaled_ff, spread_ff)
    slope = cumulative + pre_act * DENSITY_SCALE * jnp.exp(-0.5 * pre_act * pre_act)
    grad_pre = (grad_act * slope).astype(jnp.bfloat16)
    grad_fc_in = rows_product(hidden_mid, grad_pre)
    grad_bias_pre = jnp.sum(grad_pre.astype(jnp.float32), axis=0)
    grad_hidden_mid = cols_product(grad_pre, back_fc_in)
    grad_gain_two = jnp.sum(grad_hidden_mid * scaled_mid, axis=0)
    grad_shift_two = jnp.sum(grad_hidden_mid, axis=0)
    grad_mid = grad_rows + normalize_back(grad_hidden_mid, gain_back[2], scaled_mid, spread_mid)
    grad_attn_low = grad_mid.astype(jnp.bfloat16)
    grad_attn_out = rows_product(attn_low, grad_attn_low)
    grad_bias_attn = jnp.sum(grad_attn_low.astype(jnp.float32), axis=0)
    grad_normed_attn = cols_product(grad_attn_low, back_out)
    grad_gain_attn = jnp.sum(grad_normed_attn * scaled_attn, axis=0)
    grad_shift_attn = jnp.sum(grad_normed_attn, axis=0)
    grad_heads = normalize_back(grad_normed_attn, gain_back[1], scaled_attn, spread_attn)
    head_terms = jnp.sum((grad_heads * attn_mixed).reshape(row_count, HEADS, HEAD_DIM), axis=(0, 2))
    grad_head_scale = lax.psum(head_terms, ("wide", "narrow"))
    grad_mixed = (grad_heads * head_wide).astype(jnp.bfloat16)
    grad_query, grad_key, grad_value, table_terms = lax.map(
        attend_back(pair_bias(table_back), offset_table()),
        (query_blocks, key_blocks, value_blocks, grad_mixed.reshape(head_shape), log_total)
        + geometry,
    )
    grad_table = jnp.sum(table_terms, axis=0)
    grad_proj = jnp.concatenate(
        [
            grad_query.reshape(row_count, D) * QUERY_SCALE,
            grad_key.reshape(row_count, D),
            grad_value.reshape(row_count, D),
        ],
        axis=1,
    )
    grad_attn_in = rows_product(hidden_in, grad_proj)
    proj_sums = jnp.sum(grad_proj.astype(jnp.float32), axis=0)
    grad_hidden_in = cols_product(grad_proj, back_in)
    grad_gain_in = jnp.sum(grad_hidden_in * scaled_in, axis=0)
    grad_shift_in = jnp.sum(grad_hidden_in, axis=0)
    grad_tokens = (
        grad_mid + normalize_back(grad_hidden_in, gain_back[0], scaled_in, spread_in)
    ).astype(jnp.bfloat16)
    grad_gains = jnp.stack([grad_gain_in, grad_gain_attn, grad_gain_two])
    grad_biases = jnp.stack(
        [
            grad_shift_in,
            proj_sums[:D],
            proj_sums[2 * D :],
            grad_shift_attn,
            grad_bias_attn,
            grad_shift_two,
            grad_bias_out,
        ]
    )
    grad_bias_ff = jnp.stack([grad_bias_pre, grad_bias_mid])
    summed = (
        lax.psum_scatter(grad_attn_in, ("wide", "narrow"), scatter_dimension=0, tiled=True),
        lax.psum_scatter(grad_attn_out, ("wide", "narrow"), scatter_dimension=0, tiled=True),
        lax.psum_scatter(grad_fc_in, ("wide", "narrow"), scatter_dimension=0, tiled=True),
        lax.psum_scatter(grad_fc_out, ("wide", "narrow"), scatter_dimension=0, tiled=True),
        lax.psum_scatter(grad_gains, ("wide", "narrow"), scatter_dimension=1, tiled=True),
        lax.psum_scatter(grad_biases, ("wide", "narrow"), scatter_dimension=1, tiled=True),
        lax.psum_scatter(grad_gain_mid, ("wide", "narrow"), scatter_dimension=0, tiled=True),
        lax.psum_scatter(grad_bias_ff, ("wide", "narrow"), scatter_dimension=1, tiled=True),
        lax.psum_scatter(grad_table, ("wide", "narrow"), scatter_dimension=1, tiled=True),
    )
    return (
        out_tokens,
        grad_tokens,
        summed[0],
        summed[1],
        summed[2],
        summed[3],
        summed[4],
        summed[5],
        summed[6],
        summed[7],
        summed[8],
        grad_head_scale,
    )


def solution(mesh):
    placed = (
        P(("wide", "narrow"), None),
        P(("wide", "narrow"), None),
        P(("wide", "narrow"), None),
        P(("wide", "narrow"), None),
        P(("wide", "narrow"), None),
        P(("wide", "narrow"), None),
        P(None, ("wide", "narrow")),
        P(None, ("wide", "narrow")),
        P(("wide", "narrow")),
        P(None, ("wide", "narrow")),
        P(None, ("wide", "narrow")),
        P(),
        P(("wide", "narrow")),
        P(("wide", "narrow")),
    )
    return jax.shard_map(
        body,
        mesh=mesh,
        in_specs=placed,
        out_specs=(
            P(("wide", "narrow"), None),
            P(("wide", "narrow"), None),
            P(("wide", "narrow"), None),
            P(("wide", "narrow"), None),
            P(("wide", "narrow"), None),
            P(("wide", "narrow"), None),
            P(None, ("wide", "narrow")),
            P(None, ("wide", "narrow")),
            P(("wide", "narrow")),
            P(None, ("wide", "narrow")),
            P(None, ("wide", "narrow")),
            P(),
        ),
        check_vma=False,
    )
```

profile of v0, /device:TPU:0, one launch (start us, length us, event | category | flops | bytes accessed | tf_op | source)
XLA Modules:
  0.0 1394.3 jit_solution(12418934545217334785)
XLA Ops:
  14.1 43.8 %all-gather.1 = bf16[32,24,7]{1,2,0:T(8,128)(2,1)S(1)} all-gather(bf16[1,24,7]{1,2,0:T(8,128)(2,1)} %bitcast.327), channel_id=1, replica_groups=mesh['wide'=8,'narrow'=4] {'wide','narrow'}, dimensions={0}, use_global_device_ids=true | all-gather | bytes 11088 | tf_op jit(solution)/shard_map/all_gather | solution.py:229
  58.8 36.9 %all-gather = bf16[32,24,3]{1,2,0:T(4,128)(2,1)S(1)} all-gather(bf16[1,24,3]{1,2,0:T(4,128)(2,1)} %bitcast.328), channel_id=1, replica_groups=mesh['wide'=8,'narrow'=4] {'wide','narrow'}, dimensions={0}, use_global_device_ids=true | all-gather | bytes 4752 | tf_op jit(solution)/shard_map/all_gather | solution.py:228
  99.5 38.4 %all-gather.2 = bf16[32,32,12]{1,2,0:T(8,128)(2,1)S(1)} all-gather(bf16[1,32,12]{1,2,0:T(8,128)(2,1)S(1)} %bitcast.326), channel_id=1, replica_groups=mesh['wide'=8,'narrow'=4] {'wide','narrow'}, dimensions={0}, use_global_device_ids=true | all-gather | bytes 25344 | tf_op jit(solution)/shard_map/all_gather | solution.py:232
  138.6 93.3 %gather_fusion = f32[50625,12]{1,0:T(8,128)} fusion(f32[12,1024]{0,1:T(8,128)S(1)} %bitcast.289, s32[51200]{0:T(1024)S(1)} %pad_clamp_fusion), kind=kCustom, calls=%fused_computation.clone | custom fusion | bytes 5062500 | tf_op jit(solution)/shard_map/jit(_take)/gather | solution.py:80
  232.0 15.6 %copy.185 = f32[50625,12]{0,1:T(8,128)} copy(f32[50625,12]{1,0:T(8,128)} %gather_fusion) | data formatting | bytes 4860000 | tf_op jit(solution)/shard_map/jit(_take)/gather | solution.py:80
  260.6 36.5 %all-gather.3 = bf16[32,96,2]{1,2,0:T(2,128)(2,1)S(1)} all-gather(bf16[1,96,2]{1,2,0:T(2,128)(2,1)S(1)} %bitcast.329), channel_id=1, replica_groups=mesh['wide'=8,'narrow'=4] {'wide','narrow'}, dimensions={0}, use_global_device_ids=true | all-gather | bytes 12672 | tf_op jit(solution)/shard_map/all_gather | solution.py:231
  298.1 37.2 %all-reduce = bf16[3072]{0:T(1024)(128)(2,1)S(1)} all-reduce(bf16[3072]{0:T(1024)(128)(2,1)S(1)} %dynamic-update-slice), channel_id=1, replica_groups=mesh['wide'=8,'narrow'=4] {'wide','narrow'}, use_global_device_ids=true, to_apply=%add | all-reduce | flops 3072 | bytes 12288
  364.6 59.5 %while.30 = (s32[]{:T(128)}, f32[2,512,12,64]{1,3,2,0:T(8,128)}, f32[2,12,512]{2,1,0:T(8,128)S(1)}, bf16[2,512,12,64]{1,3,2,0:T(8,128)(2,1)}, s32[2,512]{1,0:T(2...) while((s32[]{:T(128)}, f32[2,512,12,64]{1,3,2,0:T(8,128)}, ...), condition=%wide.region_10.12_spmd, body=%wide.region_7.11_spmd.sunk | while | flops 13057167360 | bytes 141153200 | solution.py:264
  371.0 10.6 fusion.203
  400.5 10.6 fusion.203
  442.4 13.3 fusion.132
  460.3 16.8 %multiply_reduce_fusion.1 = (f32[3072]{0:T(1024)}, f32[1024]{0:T(1024)S(1)}, f32[1024]{0:T(1024)S(1)}, f32[3072]{0:T(1024)S(1)}, f32[1024,3072]{1,0:T(8,128)}) fusion(f32[1024,3072]{1,0:T(8,128)} %copy-done.8, f32[1024]{0:T(1024)S(1)} %add_rsqrt_fusion, f32[1024]{0:T(1024)S(1)} %broadcast_multiply_fusion.3, f32[3072]{0:T(1024)S(1)} %copy-done.41, ...), kind=kOutput, calls=%fused_computation.104 | convolution fusion | flops 4862500864 | bytes 31514624 | tf_op jit(solution)/shard_map/dot_general | solution.py:68
  477.2 13.7 convert_reduce_fusion
  490.8 12.0 fusion.138
  524.5 215.7 %while.31 = (s32[]{:T(128)}, bf16[2,512,12,64]{1,3,2,0:T(8,128)(2,1)}, bf16[2,512,12,64]{1,3,2,0:T(8,128)(2,1)}, bf16[2,512,12,64]{1,3,2,0:T(8,128)(2,1)}, f32[2...) while((s32[]{:T(128)}, ...), condition=%wide.region_25.27_spmd.clone.clone, body=%wide.region_23.26_spmd.clone.clone.sunk | while | flops 19684456448 | bytes 293369120 | solution.py:329
  532.2 8.6 fusion.225
  541.0 10.1 multiply_reduce_fusion.17
  573.1 14.2 %reshape.492 = f32[12,15,15,15,15]{2,1,4,3,0:T(8,128)} reshape(f32[12,225,225]{1,2,0:T(8,128)S(1)} %convolution_bitcast_fusion.2) | data formatting | bytes 4860000 | tf_op jit(solution)/shard_map/while/body/eval_jaxpr/reshape | solution.py:182
  587.3 38.0 %fusion.230 = f32[12,15,15,32,1]{3,1,2,4,0:T(8,128)S(1)} fusion(f32[12,15,15,15,15]{2,1,4,3,0:T(8,128)} %reshape.492, s32[15,15]{0,1:T(8,128)S(1)} %get-tuple-element.820), kind=kOutput, calls=%fused_computation.80.clone.1 | convolution fusion | flops 233294400 | bytes 2776500 | tf_op jit(solution)/shard_map/while/body/eval_jaxpr/hrcsd,rsa->hacd/dot_general | solution.py:183
  634.8 8.5 fusion.225
  643.7 10.1 multiply_reduce_fusion.17
  675.4 14.2 %reshape.492 = f32[12,15,15,15,15]{2,1,4,3,0:T(8,128)} reshape(f32[12,225,225]{1,2,0:T(8,128)S(1)} %convolution_bitcast_fusion.2) | data formatting | bytes 4860000 | tf_op jit(solution)/shard_map/while/body/eval_jaxpr/reshape | solution.py:182
  689.6 38.0 %fusion.230 = f32[12,15,15,32,1]{3,1,2,4,0:T(8,128)S(1)} fusion(f32[12,15,15,15,15]{2,1,4,3,0:T(8,128)} %reshape.492, s32[15,15]{0,1:T(8,128)S(1)} %get-tuple-element.820), kind=kOutput, calls=%fused_computation.80.clone.1 | convolution fusion | flops 233294400 | bytes 2776500 | tf_op jit(solution)/shard_map/while/body/eval_jaxpr/hrcsd,rsa->hacd/dot_general | solution.py:183
  765.9 10.6 fusion.129
  777.9 10.4 fusion.109
  789.0 9.1 multiply_convert_fusion.2
  799.8 9.1 fusion.137
  823.6 43.3 %all-reduce.4 = (f32[3,768]{1,0:T(4,128)S(1)}, f32[7,768]{1,0:T(8,128)S(1)}, f32[3072]{0:T(1024)S(1)}, f32[12]{0:T(128)}) all-reduce(f32[3,768]{1,0:T(4,128)S(1)} %pad_maximum_fusion.1, f32[7,768]{1,0:T(8,128)S(1)} %stack.56, f32[3072]{0:T(1024)S(1)} %copy-done.68, ...), channel_id=6, replica_groups=mesh['wide'=8,'narrow'=4] {'wide','narrow'}, use_global_device_ids=true, to_apply=%region_35.37.clone | all-reduce | flops 10764 | bytes 86112
  879.1 100.3 %reduce-scatter.15.cloned.1.call-done = f32[24,768]{1,0:T(8,128)} async-done(((f32[768,768]{1,0:T(8,128)}), f32[24,768]{1,0:T(8,128)}) %reduce-scatter.15.cloned.1.call-update) | async-done | bytes 73744 | tf_op jit(solution)/shard_map/reduce_scatter | solution.py:366
  979.5 124.4 %reduce-scatter.13.cloned.1.call-done = f32[24,2304]{1,0:T(8,128)} async-done(((f32[768,2304]{1,0:T(8,128)}), f32[24,2304]{1,0:T(8,128)}) %reduce-scatter.13.cloned.1.call-update) | async-done | bytes 221200 | tf_op jit(solution)/shard_map/reduce_scatter | solution.py:365
  1103.9 142.4 %reduce-scatter.17.cloned.1.call-done = f32[24,3072]{1,0:T(8,128)} async-done(((f32[768,3072]{1,0:T(8,128)}), f32[24,3072]{1,0:T(8,128)}) %reduce-scatter.17.cloned.1.call-update) | async-done | bytes 294928 | tf_op jit(solution)/shard_map/reduce_scatter | solution.py:367
  1246.3 140.9 %reduce-scatter.19.cloned.1.call-done = f32[96,768]{1,0:T(8,128)} async-done(((f32[3072,768]{1,0:T(8,128)}), f32[96,768]{1,0:T(8,128)}) %reduce-scatter.19.cloned.1.call-update) | async-done | bytes 294928 | tf_op jit(solution)/shard_map/reduce_scatter | solution.py:368
  (411 shorter events, 255.7 us)
Async XLA Ops:
  7.2 331.4 %all-gather.9.cloned.1.call-start = ((), (), s32[]{:S(2)}) async-start(), calls=%async_computation.6 | async-start | bytes 3649536 | tf_op jit(solution)/shard_map/all_gather | solution.py:224
  7.9 428.1 %all-gather.11.cloned.1.call-start = ((), (), s32[]{:S(2)}) async-start(), calls=%async_computation.7 | async-start | bytes 1216512 | tf_op jit(solution)/shard_map/all_gather | solution.py:225
  8.7 433.7 %all-gather.13.cloned.1.call-start = ((), (), s32[]{:S(2)}) async-start(), calls=%async_computation.8 | async-start | bytes 4866048 | tf_op jit(solution)/shard_map/all_gather | solution.py:226
  9.4 450.9 %all-gather.15.cloned.1.call-start = ((), (), s32[]{:S(2)}) async-start(), calls=%async_computation.9 | async-start | bytes 4866048 | tf_op jit(solution)/shard_map/all_gather | solution.py:227
  10.0 858.8 %reduce-scatter.21.cloned.1.call-start = ((), (), s32[]{:S(2)}) async-start(), calls=%async_computation.14 | async-start | bytes 1622016
  58.8 279.7 %copy-start.73 = (f32[768]{0:T(1024)}, f32[768]{0:T(1024)S(1)}, u32[]{:S(2)}) copy-start(f32[768]{0:T(1024)S(1)} %get-tuple-element.452) | copy-start | bytes 9220
  96.6 241.9 %copy-start.56 = (f32[768]{0:T(1024)}, f32[768]{0:T(1024)S(1)}, u32[]{:S(2)}) copy-start(f32[768]{0:T(1024)S(1)} %get-tuple-element.455) | copy-start | bytes 9220
  98.4 240.2 %copy-start.10 = (bf16[1024,768]{0,1:T(8,128)(2,1)}, bf16[1024,768]{0,1:T(8,128)(2,1)S(1)}, u32[]{:S(2)}) copy-start(bf16[1024,768]{0,1:T(8,128)(2,1)S(1)} %copy.174) | copy-start | bytes 4718596
  98.6 239.9 %copy-start.37 = (f32[1024]{0:T(1024)}, f32[1024]{0:T(1024)S(1)}, u32[]{:S(2)}) copy-start(f32[1024]{0:T(1024)S(1)} %broadcast_multiply_fusion.12) | copy-start | bytes 12292
  99.1 239.4 %copy-start.52 = (f32[1024]{0:T(1024)}, f32[1024]{0:T(1024)S(1)}, u32[]{:S(2)}) copy-start(f32[1024]{0:T(1024)S(1)} %add_rsqrt_fusion.2) | copy-start | bytes 12292
  255.9 42.0 %copy-start.82 = (bf16[96]{0:T(256)(128)(2,1)S(1)}, bf16[96]{0:T(256)(128)(2,1)}, u32[]{:S(2)}) copy-start(bf16[96]{0:T(256)(128)(2,1)} %param.28) | copy-start | bytes 580
  429.8 85.4 %copy-start.46 = (f32[1,4,2,128]{3,1,2,0:T(4,128)}, f32[1,4,2,128]{3,1,2,0:T(4,128)S(1)}, u32[]{:S(2)}) copy-start(f32[1,4,2,128]{3,1,2,0:T(4,128)S(1)} %copy.233) | copy-start | bytes 12292
  429.8 85.4 %copy-start.48 = (f32[1,4,2,128]{3,1,2,0:T(4,128)}, f32[1,4,2,128]{3,1,2,0:T(4,128)S(1)}, u32[]{:S(2)}) copy-start(f32[1,4,2,128]{3,1,2,0:T(4,128)S(1)} %copy.232) | copy-start | bytes 12292
  440.2 70.2 %copy-start.39 = (f32[1024]{0:T(1024)}, f32[1024]{0:T(1024)S(1)}, u32[]{:S(2)}) copy-start(f32[1024]{0:T(1024)S(1)} %broadcast_multiply_fusion.11) | copy-start | bytes 12292
  442.3 68.2 %copy-start.54 = (f32[1024]{0:T(1024)}, f32[1024]{0:T(1024)S(1)}, u32[]{:S(2)}) copy-start(f32[1024]{0:T(1024)S(1)} %add_rsqrt_fusion.1) | copy-start | bytes 12292
  460.3 16.9 %copy-start.42 = (f32[1,3072]{1,0:T(1,128)S(1)}, f32[1,3072]{1,0:T(1,128)}, u32[]{:S(2)}) copy-start(f32[1,3072]{1,0:T(1,128)} %get-tuple-element.536) | copy-start | bytes 36868
  460.3 16.8 %copy-start.9 = (f32[1024,3072]{1,0:T(8,128)S(1)}, f32[1024,3072]{1,0:T(8,128)}, u32[]{:S(2)}) copy-start(f32[1024,3072]{1,0:T(8,128)} %copy-done.8) | copy-start | bytes 37748740
  490.8 12.0 copy-start.21
  524.4 353.4 %reduce-scatter.23.cloned.1.call-start = ((), (), s32[]{:S(2)}) async-start(), calls=%async_computation.15 | async-start | bytes 540672
  524.4 217.8 %copy-start.45 = (f32[768]{0:T(1024)S(1)}, f32[768]{0:T(1024)}, u32[]{:S(2)}) copy-start(f32[768]{0:T(1024)} %mul.312) | copy-start | bytes 9220
  524.4 217.8 %copy-start.47 = (f32[1,4,2,128]{3,1,2,0:T(4,128)S(1)}, f32[1,4,2,128]{3,1,2,0:T(4,128)}, u32[]{:S(2)}) copy-start(f32[1,4,2,128]{3,1,2,0:T(4,128)} %copy-done.46) | copy-start | bytes 12292
  524.5 217.8 %copy-start.49 = (f32[1,4,2,128]{3,1,2,0:T(4,128)S(1)}, f32[1,4,2,128]{3,1,2,0:T(4,128)}, u32[]{:S(2)}) copy-start(f32[1,4,2,128]{3,1,2,0:T(4,128)} %copy-done.48) | copy-start | bytes 12292
  524.5 217.8 %copy-start.51 = (f32[768]{0:T(1024)S(1)}, f32[768]{0:T(1024)}, u32[]{:S(2)}) copy-start(f32[768]{0:T(1024)} %get-tuple-element.454) | copy-start | bytes 9220
  524.5 217.8 %copy-start.76 = (f32[768]{0:T(1024)S(1)}, f32[768]{0:T(1024)}, u32[]{:S(2)}) copy-start(f32[768]{0:T(1024)} %get-tuple-element.449) | copy-start | bytes 9220
  587.3 40.7 %copy-start.35 = (f32[2,12,1024]{2,1,0:T(8,128)S(1)}, f32[2,12,1024]{2,1,0:T(8,128)}, u32[]{:S(2)}) copy-start(f32[2,12,1024]{2,1,0:T(8,128)} %get-tuple-element.792) | copy-start | bytes 294916 | tf_op jit(solution)/shard_map/while
  587.3 41.4 %copy-start.7 = (bf16[2,512,12,64]{1,3,2,0:T(8,128)(2,1)S(1)}, bf16[2,512,12,64]{1,3,2,0:T(8,128)(2,1)}, u32[]{:S(2)}) copy-start(bf16[2,512,12,64]{1,3,2,0:T(8,128)(2,1)} %copy-done.6) | copy-start | bytes 4718596 | tf_op jit(solution)/shard_map/while
  689.6 40.7 %copy-start.35 = (f32[2,12,1024]{2,1,0:T(8,128)S(1)}, f32[2,12,1024]{2,1,0:T(8,128)}, u32[]{:S(2)}) copy-start(f32[2,12,1024]{2,1,0:T(8,128)} %get-tuple-element.792) | copy-start | bytes 294916 | tf_op jit(solution)/shard_map/while
  689.6 41.4 %copy-start.7 = (bf16[2,512,12,64]{1,3,2,0:T(8,128)(2,1)S(1)}, bf16[2,512,12,64]{1,3,2,0:T(8,128)(2,1)}, u32[]{:S(2)}) copy-start(bf16[2,512,12,64]{1,3,2,0:T(8,128)(2,1)} %copy-done.6) | copy-start | bytes 4718596 | tf_op jit(solution)/shard_map/while
  742.2 237.3 %reduce-scatter.15.cloned.1.call-start = ((), (), s32[]{:S(2)}) async-start(), calls=%async_computation.11 | async-start | bytes 2433024 | tf_op jit(solution)/shard_map/reduce_scatter | solution.py:366
  748.4 355.5 %reduce-scatter.13.cloned.1.call-start = ((), (), s32[]{:S(2)}) async-start(), calls=%async_computation.10 | async-start | bytes 7299072 | tf_op jit(solution)/shard_map/reduce_scatter | solution.py:365
  765.2 481.1 %reduce-scatter.17.cloned.1.call-start = ((), (), s32[]{:S(2)}) async-start(), calls=%async_computation.12 | async-start | bytes 9732096 | tf_op jit(solution)/shard_map/reduce_scatter | solution.py:367
  776.5 610.8 %reduce-scatter.19.cloned.1.call-start = ((), (), s32[]{:S(2)}) async-start(), calls=%async_computation.13 | async-start | bytes 9732096 | tf_op jit(solution)/shard_map/reduce_scatter | solution.py:368
  (77 other events, 270.6 us)
Sparse Core Ops, SparseCore 0:
  10.9 62.8 all-gather.8
  76.7 52.9 all-gather.10
  132.7 62.5 all-gather.12
  198.0 62.4 all-gather.14
  524.5 98.4 reduce-scatter.20
  742.3 135.4 reduce-scatter.22
  884.5 94.9 reduce-scatter.14
  985.7 118.1 reduce-scatter.12
  1111.4 134.9 reduce-scatter.16
  1252.7 134.5 reduce-scatter.18
where the time goes:
time: 1400 us; the launch traced here: 1390 us
  waiting for transfers between devices  518 us (37%)
  matrix products  301 us (22%)
  blocking collectives  236 us (17%)
  local copies, waits for them, and re-layouts  234 us (17%)
  other arithmetic  76.1 us (5%)
  between operations  15.6 us (1%)
    reduce_scatter x1, waiting for transfers between devices, body(): lax.psum_scatter(grad_fc_in, ('wide', 'narrow'), scatter_dimension=0, til...  142 us
    reduce_scatter x1, waiting for transfers between devices, body(): lax.psum_scatter(grad_fc_out, ('wide', 'narrow'), scatter_dimension=0, ti...  141 us
    reduce_scatter x1, waiting for transfers between devices, body(): lax.psum_scatter(grad_attn_in, ('wide', 'narrow'), scatter_dimension=0, t...  124 us
    gather x3, local copies, waits for them, and re-layouts, pair_bias(): return jnp.take(bias_table, pair_index, axis=1)  114 us
    reduce_scatter x1, waiting for transfers between devices, body(): lax.psum_scatter(grad_attn_out, ('wide', 'narrow'), scatter_dimension=0,...  100 us
    unnamed x2, blocking collectives  80.5 us
    dot_general x2, matrix products, back_block(): jnp.einsum('hrcsd,rsa->hacd', by_pair, shifts, precision=PRECISE, preferr...  76.1 us
    all_gather x1, blocking collectives, body(): lax.all_gather(biases_d, ('wide', 'narrow'), axis=1, tiled=True)  43.8 us
  transfers between devices with their start and end apart: 10, of which 5 were waited for; matrix products, arithmetic and copies ran while one was open for 38% of the time, Pallas kernels for 0%

commit v1 on v0

v1 whole, which is shorter than its diff:
```python
import functools

import jax
import jax.numpy as jnp
import numpy as np
from jax import lax
from jax.experimental import pallas as pl
from jax.experimental.pallas import tpu as pltpu
from jax.sharding import PartitionSpec as P

HEADS = 12
HEAD_DIM = 64
D = 768
FF = 3072
GRID_L = 15
GRID_S = 8
SLOT_L = 256
SLOT_S = 64
STRIDE = 32
RELS = 1024
CHUNK = 256
PIECES = 16
ROWS_D = D // PIECES
ROWS_F = FF // (2 * PIECES)

NEG_FILL = -1e30
NORM_EPS = 1e-05
HALF_ROOT = 0.7071067811865476
DENSITY_SCALE = 0.3989422804014327
QUERY_SCALE = 0.125
AXES = ("wide", "narrow")
F32 = jnp.float32
BF16 = jnp.bfloat16
VMEM_BIG = 60 * 2**20

NN = (((1,), (0,)), ((), ()))
NT = (((1,), (1,)), ((), ()))
TN = (((0,), (0,)), ((), ()))


def dot(left, right, dims=NN):
    return lax.dot_general(left, right, dims, preferred_element_type=F32)


def unit_rows(values):
    center = values - jnp.mean(values, axis=-1, keepdims=True)
    spread = lax.rsqrt(jnp.mean(center * center, axis=-1, keepdims=True) + NORM_EPS)
    return center * spread, spread


def unit_rows_back(inner, scaled, spread):
    return spread * (
        inner
        - jnp.mean(inner, axis=-1, keepdims=True)
        - scaled * jnp.mean(inner * scaled, axis=-1, keepdims=True)
    )


def col_sum(values):
    return jnp.sum(values, axis=0, keepdims=True)


def unit_position(kind):
    place = np.arange(CHUNK)
    if kind == 0:
        return np.minimum(place // GRID_L, GRID_L - 1), place % GRID_L
    inner = place % SLOT_S
    return inner // GRID_S, inner % GRID_S


def pick_tables():
    keys = np.zeros((2, CHUNK, 512), np.float32)
    keys_back = np.zeros((2, CHUNK, 512), np.float32)
    queries = np.zeros((2, CHUNK, CHUNK), np.float32)
    for kind in range(2):
        row, col = unit_position(kind)
        line = STRIDE * row + col
        keys[kind, np.arange(CHUNK), line] = 1
        keys_back[kind, np.arange(CHUNK), 511 - line] = 1
        queries[kind, 16 * row + col, np.arange(CHUNK)] = 1
    return keys.astype(BF16), keys_back.astype(BF16), queries.astype(BF16)


def bias_kernel(table_ref, keys_ref, queries_ref, out_ref):
    line = jnp.broadcast_to(table_ref[0], (16, RELS))
    base = pltpu.roll(line, RELS - 511, 1, stride=1, stride_axis=0)
    groups = [base[:, :512]]
    for r in range(1, 16):
        groups.append(pltpu.roll(base, STRIDE * r, 1)[:, :512])
    spread_rows = jnp.concatenate(groups, axis=0).astype(BF16)
    for kind in range(2):
        by_key = dot(keys_ref[kind], spread_rows, NT).astype(BF16)
        tile = dot(by_key, queries_ref[kind])
        if kind == 1:
            left = lax.broadcasted_iota(jnp.int32, (CHUNK, CHUNK), 0) // SLOT_S
            right = lax.broadcasted_iota(jnp.int32, (CHUNK, CHUNK), 1) // SLOT_S
            tile = jnp.where(left == right, tile, NEG_FILL)
        out_ref[kind, 0] = tile.astype(BF16)


def build_bias(flipped, keys, queries):
    return pl.pallas_call(
        bias_kernel,
        grid=(HEADS,),
        in_specs=[
            pl.BlockSpec((1, 1, RELS), lambda h: (h, 0, 0)),
            pl.BlockSpec((2, CHUNK, 512), lambda h: (0, 0, 0)),
            pl.BlockSpec((2, CHUNK, CHUNK), lambda h: (0, 0, 0)),
        ],
        out_specs=pl.BlockSpec((2, 1, CHUNK, CHUNK), lambda h: (0, h, 0, 0)),
        out_shape=jax.ShapeDtypeStruct((2, HEADS, CHUNK, CHUNK), BF16),
        compiler_params=pltpu.CompilerParams(vmem_limit_bytes=VMEM_BIG),
        name="bias_tiles",
    )(flipped, keys, queries)


def halves(values):
    high = values.astype(BF16)
    return high, (values - high.astype(F32)).astype(BF16)


def table_kernel(tiles_ref, keys_ref, queries_ref, out_ref):
    total = jnp.zeros((CHUNK, 512), F32)
    for kind in range(2):
        high, rest = halves(tiles_ref[kind, 0])
        by_query = dot(queries_ref[kind], high, NT) + dot(queries_ref[kind], rest, NT)
        high, rest = halves(by_query)
        total = total + dot(high, keys_ref[kind]) + dot(rest, keys_ref[kind])
    wide = jnp.concatenate([total, jnp.zeros((CHUNK, 512), F32)], axis=1)
    line = wide[:16]
    for r in range(1, 15):
        line = line + pltpu.roll(wide[16 * r : 16 * r + 16], STRIDE * r, 1)
    line = pltpu.roll(line, 0, 1, stride=1, stride_axis=0)
    out_ref[0] = pltpu.roll(jnp.broadcast_to(col_sum(line), (8, RELS)), RELS - 16, 1)


def table_grads(tiles, keys_back, queries):
    return pl.pallas_call(
        table_kernel,
        grid=(HEADS,),
        in_specs=[
            pl.BlockSpec((2, 1, CHUNK, CHUNK), lambda h: (0, h, 0, 0)),
            pl.BlockSpec((2, CHUNK, 512), lambda h: (0, 0, 0)),
            pl.BlockSpec((2, CHUNK, CHUNK), lambda h: (0, 0, 0)),
        ],
        out_specs=pl.BlockSpec((1, 8, RELS), lambda h: (h, 0, 0)),
        out_shape=jax.ShapeDtypeStruct((HEADS, 8, RELS), F32),
        compiler_params=pltpu.CompilerParams(vmem_limit_bytes=VMEM_BIG),
        name="table_grads",
    )(tiles, keys_back, queries)[:, 0]


META_KIND = 1
META_FROM = {"a": 8, "b": 24}
META_TO = {"a": 40, "b": 56}


class Load:
    def __init__(self, meta, sem, scratch):
        self.meta, self.sem, self.scratch = meta, sem, scratch

    def cols(self, order, own, other, start):
        core, rows = self.meta[0], own.shape[1]
        for k in range(PIECES):
            place = pl.multiple_of(self.meta[META_FROM[order] + k] * rows, 16)
            for half, source in ((core, own), (1 - core, other)):
                pltpu.make_async_copy(
                    source.at[k],
                    self.scratch.at[half, pl.ds(place, rows), pl.ds(start, own.shape[2])],
                    self.sem,
                ).start()

    def rows(self, order, own, other):
        core, rows = self.meta[0], own.shape[1]
        for k in range(PIECES):
            chip = self.meta[META_FROM[order] + k]
            for half, source in ((core, own), (1 - core, other)):
                place = pl.multiple_of((2 * chip + half) * rows, 16)
                pltpu.make_async_copy(
                    source.at[k], self.scratch.at[pl.ds(place, rows)], self.sem
                ).start()

    def wait(self):
        pltpu.make_async_copy(self.scratch, self.scratch, self.sem).wait()


ANY = pl.BlockSpec(memory_space=pl.ANY)


def full(*shape):
    return pl.BlockSpec(shape, lambda *_: (0,) * len(shape))


def attend_kernel(
    meta, x_ref, vec_ref, a0, a1, b0, b1, bias_ref, mask_ref,
    low_ref, q_ref, k_ref, v_ref, mixed_ref, turned_ref, lse_ref, w_scr, sem,
):
    @pl.when(pl.program_id(0) == 0)
    def _():
        load = Load(meta, sem, w_scr)
        load.cols("a", a0, a1, 0)
        load.cols("b", b0, b1, a0.shape[2])
        load.wait()

    scaled, _ = unit_rows(x_ref[...].astype(F32))
    low = (scaled * vec_ref[0:1] + vec_ref[3:4]).astype(BF16)
    low_ref[...] = low
    first = dot(low, w_scr[0])
    second = dot(low, w_scr[1])
    query = (first[:, :D] + vec_ref[4:5]) * QUERY_SCALE
    query_turned = query.T.astype(BF16)
    q_ref[...] = query.astype(BF16)
    k_ref[...] = jnp.concatenate([first[:, D:], second[:, : D // 2]], axis=1).astype(BF16)
    value = second[:, D // 2 :] + vec_ref[5:6]
    value_turned = value.T.astype(BF16)
    v_ref[...] = value.astype(BF16)
    mask = jnp.broadcast_to(mask_ref[...], (CHUNK, CHUNK))
    sums = []
    for h in range(HEADS):
        part = slice(h * HEAD_DIM, (h + 1) * HEAD_DIM)
        scores = dot(k_ref[:, part], query_turned[part]) + bias_ref[0, h].astype(F32) + mask
        largest = jnp.max(scores, axis=0, keepdims=True)
        exponent = jnp.exp(scores - largest)
        row_total = jnp.sum(exponent, axis=0, keepdims=True)
        out = dot(value_turned[part], exponent.astype(BF16))
        turned_ref[0, part] = out * (1.0 / row_total)
        sums.append(largest + jnp.log(row_total))
    lse_ref[0] = jnp.concatenate(sums + [jnp.zeros((16 - HEADS, CHUNK), F32)], axis=0)
    mixed_ref[...] = turned_ref[0].T


def attend(meta, tokens, vec, w_in, bias, mask):
    rows = tokens.shape[0]
    chunks = rows // CHUNK
    tile = pl.BlockSpec((CHUNK, D), lambda c, m: (c, 0))
    return pl.pallas_call(
        attend_kernel,
        grid_spec=pltpu.PrefetchScalarGridSpec(
            num_scalar_prefetch=1,
            grid=(chunks,),
            in_specs=[
                tile,
                full(16, D),
                ANY, ANY, ANY, ANY,
                pl.BlockSpec((1, HEADS, CHUNK, CHUNK), lambda c, m: (m[META_KIND + c], 0, 0, 0)),
                pl.BlockSpec((CHUNK, 1), lambda c, m: (c, 0)),
            ],
            out_specs=[
                tile, tile, tile, tile, tile,
                pl.BlockSpec((1, D, CHUNK), lambda c, m: (c, 0, 0)),
                pl.BlockSpec((1, 16, CHUNK), lambda c, m: (c, 0, 0)),
            ],
            scratch_shapes=[pltpu.VMEM((2, D, 3 * D // 2), BF16), pltpu.SemaphoreType.DMA],
        ),
        out_shape=[jax.ShapeDtypeStruct((rows, D), BF16)] * 4
        + [
            jax.ShapeDtypeStruct((rows, D), F32),
            jax.ShapeDtypeStruct((chunks, D, CHUNK), F32),
            jax.ShapeDtypeStruct((chunks, 16, CHUNK), F32),
        ],
        compiler_params=pltpu.CompilerParams(vmem_limit_bytes=VMEM_BIG),
        cost_estimate=pl.CostEstimate(
            flops=2 * rows * D * 3 * D, bytes_accessed=24 * rows * D, transcendentals=0
        ),
        name="attend",
    )(meta, tokens, vec, *w_in, bias, mask)


SUB = 16


def feed_kernel(
    meta, x_ref, mixed_ref, cot_ref, live_ref, vec_ref, wide_ref,
    o0, o1, i0, i1, f0, f1,
    out_ref, mid_ref, aln_ref, low_ref, m_ref, dz_ref, df_ref, sums_ref, sums_ff_ref,
    wo_scr, wi_scr, wf_scr, z_scr, unit_scr, dm_scr, spread_scr, acc_scr, sems,
):
    step = pl.program_id(0)

    @pl.when(step == 0)
    def _():
        loads = [Load(meta, sems.at[i], s) for i, s in enumerate((wo_scr, wi_scr, wf_scr))]
        loads[0].cols("a", o0, o1, 0)
        loads[1].cols("a", i0, i1, 0)
        loads[2].rows("b", f0, f1)
        for load in loads:
            load.wait()
        acc_scr[...] = jnp.zeros_like(acc_scr)
        sums_ref[...] = jnp.zeros_like(sums_ref)

    live = live_ref[...]
    scaled, _ = unit_rows(mixed_ref[...] * vec_ref[10:11])
    aln = (scaled * vec_ref[1:2] + vec_ref[6:7]).astype(BF16)
    aln_ref[...] = aln
    branch = jnp.concatenate([dot(aln, wo_scr[0]), dot(aln, wo_scr[1])], axis=1)
    mid = x_ref[...].astype(F32) + branch + vec_ref[7:8]
    mid_ref[...] = mid
    scaled, _ = unit_rows(mid)
    low = (scaled * vec_ref[2:3] + vec_ref[8:9]).astype(BF16)
    low_ref[...] = low
    for half in range(2):
        part = slice(half * FF // 2, (half + 1) * FF // 2)
        z_scr[:, part] = dot(low, wi_scr[half]) + wide_ref[1:2, part]

    def forward(i, carry):
        rows = pl.ds(i * SUB, SUB)
        z = z_scr[rows]
        cumulative = 0.5 * (1.0 + lax.erf(z * HALF_ROOT))
        unit, spread = unit_rows(z * cumulative)
        z_scr[rows] = cumulative + z * (DENSITY_SCALE * jnp.exp(-0.5 * z * z))
        unit_scr[rows] = unit
        spread_scr[rows] = jnp.broadcast_to(spread, (SUB, 128))
        m_ref[rows] = (unit * wide_ref[0:1] + wide_ref[2:3]).astype(BF16)
        return carry

    lax.fori_loop(0, CHUNK // SUB, forward, 0)
    out = mid + dot(m_ref[...], wf_scr[...]) + vec_ref[9:10]
    out_ref[...] = (out * live).astype(BF16)
    df_full = cot_ref[...].astype(F32) * live
    df = df_full.astype(BF16)
    df_ref[...] = df
    sums_ref[0:1] += col_sum(df_full)
    dm_scr[...] = dot(df, wf_scr[...], NT)

    def backward(i, carry):
        rows = pl.ds(i * SUB, SUB)
        dm = dm_scr[rows]
        unit = unit_scr[rows]
        acc_scr[0] += dm * unit
        acc_scr[1] += dm
        du = unit_rows_back(dm * wide_ref[0:1], unit, spread_scr[rows, 0:1])
        dz_full = du * z_scr[rows]
        dz = dz_full.astype(BF16)
        acc_scr[2] += dz_full
        dz_ref[0, rows] = dz[:, : FF // 2]
        dz_ref[1, rows] = dz[:, FF // 2 :]
        return carry

    lax.fori_loop(0, CHUNK // SUB, backward, 0)

    @pl.when(step == pl.num_programs(0) - 1)
    def _():
        sums_ff_ref[...] = jnp.sum(acc_scr[...], axis=1)


def feed(meta, tokens, mixed, cot, live, vec, wide, w_out, w_in, w_down):
    rows = tokens.shape[0]
    tile = pl.BlockSpec((CHUNK, D), lambda c, m: (c, 0))
    return pl.pallas_call(
        feed_kernel,
        grid_spec=pltpu.PrefetchScalarGridSpec(
            num_scalar_prefetch=1,
            grid=(rows // CHUNK,),
            in_specs=[
                tile, tile, tile,
                pl.BlockSpec((CHUNK, 1), lambda c, m: (c, 0)),
                full(16, D), full(8, FF),
                ANY, ANY, ANY, ANY, ANY, ANY,
            ],
            out_specs=[
                tile, tile, tile, tile,
                pl.BlockSpec((CHUNK, FF), lambda c, m: (c, 0)),
                pl.BlockSpec((2, CHUNK, FF // 2), lambda c, m: (0, c, 0)),
                tile,
                full(8, D),
                full(3, FF),
            ],
            scratch_shapes=[
                pltpu.VMEM((2, D, D // 2), BF16),
                pltpu.VMEM((2, D, FF // 2), BF16),
                pltpu.VMEM((FF, D), BF16),
                pltpu.VMEM((CHUNK, FF), F32),
                pltpu.VMEM((CHUNK, FF), F32),
                pltpu.VMEM((CHUNK, FF), F32),
                pltpu.VMEM((CHUNK, 128), F32),
                pltpu.VMEM((3, SUB, FF), F32),
                pltpu.SemaphoreType.DMA((3,)),
            ],
        ),
        out_shape=[
            jax.ShapeDtypeStruct((rows, D), BF16),
            jax.ShapeDtypeStruct((rows, D), F32),
            jax.ShapeDtypeStruct((rows, D), BF16),
            jax.ShapeDtypeStruct((rows, D), BF16),
            jax.ShapeDtypeStruct((rows, FF), BF16),
            jax.ShapeDtypeStruct((2, rows, FF // 2), BF16),
            jax.ShapeDtypeStruct((rows, D), BF16),
            jax.ShapeDtypeStruct((8, D), F32),
            jax.ShapeDtypeStruct((3, FF), F32),
        ],
        compiler_params=pltpu.CompilerParams(vmem_limit_bytes=VMEM_BIG),
        cost_estimate=pl.CostEstimate(
            flops=2 * rows * D * (D + 3 * FF), bytes_accessed=40 * rows * D, transcendentals=0
        ),
        name="feed",
    )(meta, tokens, mixed, cot, live, vec, wide, *w_out, *w_in, *w_down)


def middle_kernel(
    meta, dz_ref, mid_ref, mixed_ref, cot_ref, live_ref, vec_ref, i0, i1, o0, o1,
    da_ref, dx_ref, do_ref, sums_ref, wi_scr, wo_scr, sems,
):
    @pl.when(pl.program_id(0) == 0)
    def _():
        loads = [Load(meta, sems.at[i], s) for i, s in enumerate((wi_scr, wo_scr))]
        loads[0].cols("a", i0, i1, 0)
        loads[1].cols("a", o0, o1, 0)
        for load in loads:
            load.wait()
        sums_ref[...] = jnp.zeros_like(sums_ref)

    dh = dot(dz_ref[0], wi_scr[0], NT) + dot(dz_ref[1], wi_scr[1], NT)
    scaled, spread = unit_rows(mid_ref[...])
    sums_ref[0:1] += col_sum(dh * scaled)
    sums_ref[1:2] += col_sum(dh)
    dx = cot_ref[...].astype(F32) * live_ref[...] + unit_rows_back(dh * vec_ref[2:3], scaled, spread)
    dx_ref[...] = dx
    sums_ref[2:3] += col_sum(dx)
    da = dx.astype(BF16)
    da_ref[0] = da[:, : D // 2]
    da_ref[1] = da[:, D // 2 :]
    dn = dot(da[:, : D // 2], wo_scr[0], NT) + dot(da[:, D // 2 :], wo_scr[1], NT)
    mixed = mixed_ref[...]
    scaled, spread = unit_rows(mixed * vec_ref[10:11])
    sums_ref[3:4] += col_sum(dn * scaled)
    sums_ref[4:5] += col_sum(dn)
    heads = unit_rows_back(dn * vec_ref[1:2], scaled, spread)
    sums_ref[5:6] += col_sum(heads * mixed)
    do_ref[...] = (heads * vec_ref[10:11]).astype(BF16)


def middle(meta, dz, mid, mixed, cot, live, vec, w_in, w_out):
    rows = mid.shape[0]
    tile = pl.BlockSpec((CHUNK, D), lambda c, m: (c, 0))
    return pl.pallas_call(
        middle_kernel,
        grid_spec=pltpu.PrefetchScalarGridSpec(
            num_scalar_prefetch=1,
            grid=(rows // CHUNK,),
            in_specs=[
                pl.BlockSpec((2, CHUNK, FF // 2), lambda c, m: (0, c, 0)),
                tile, tile, tile,
                pl.BlockSpec((CHUNK, 1), lambda c, m: (c, 0)),
                full(16, D),
                ANY, ANY, ANY, ANY,
            ],
            out_specs=[
                pl.BlockSpec((2, CHUNK, D // 2), lambda c, m: (0, c, 0)),
                tile, tile,
                full(8, D),
            ],
            scratch_shapes=[
                pltpu.VMEM((2, D, FF // 2), BF16),
                pltpu.VMEM((2, D, D // 2), BF16),
                pltpu.SemaphoreType.DMA((2,)),
            ],
        ),
        out_shape=[
            jax.ShapeDtypeStruct((2, rows, D // 2), BF16),
            jax.ShapeDtypeStruct((rows, D), F32),
            jax.ShapeDtypeStruct((rows, D), BF16),
            jax.ShapeDtypeStruct((8, D), F32),
        ],
        compiler_params=pltpu.CompilerParams(vmem_limit_bytes=VMEM_BIG),
        cost_estimate=pl.CostEstimate(
            flops=2 * rows * D * (D + FF), bytes_accessed=30 * rows * D, transcendentals=0
        ),
        name="middle",
    )(meta, dz, mid, mixed, cot, live, vec, *w_in, *w_out)


def attend_back_kernel(
    meta, q_ref, k_ref, v_ref, do_ref, turned_ref, lse_ref, bias_ref, mask_ref,
    dqkv_ref, tiles_ref, dq_scr, do_scr,
):
    step = pl.program_id(0)
    kind = meta[META_KIND + step]

    @pl.when(step == 0)
    def _():
        tiles_ref[...] = jnp.zeros_like(tiles_ref)

    query = q_ref[...]
    query_turned = query.astype(F32).T.astype(BF16)
    key_turned = k_ref[...].astype(F32).T.astype(BF16)
    do_scr[...] = do_ref[...].astype(F32).T
    mask = jnp.broadcast_to(mask_ref[...], (CHUNK, CHUNK))
    dk, dv = [], []
    for h in range(HEADS):
        part = slice(h * HEAD_DIM, (h + 1) * HEAD_DIM)
        key, value = k_ref[:, part], v_ref[:, part]
        do_turned = do_scr[part]
        scores = dot(key, query_turned[part]) + bias_ref[0, h].astype(F32) + mask
        probs = jnp.exp(scores - lse_ref[0, h : h + 1])
        centre = jnp.sum(do_turned * turned_ref[0, part], axis=0, keepdims=True)
        ds_full = probs * (dot(value, do_turned.astype(BF16)) - centre)
        ds = ds_full.astype(BF16)
        tiles_ref[kind, h] += ds_full
        dv.append(dot(probs.astype(BF16), do_ref[:, part]))
        dk.append(dot(ds, q_ref[:, part]))
        dq_scr[part] = dot(key_turned[part], ds)
    dq = (dq_scr[...].T * QUERY_SCALE).astype(BF16)
    dk = jnp.concatenate(dk, axis=1).astype(BF16)
    dv = jnp.concatenate(dv, axis=1).astype(BF16)
    dqkv_ref[0, :, :D] = dq
    dqkv_ref[0, :, D:] = dk[:, : D // 2]
    dqkv_ref[1, :, : D // 2] = dk[:, D // 2 :]
    dqkv_ref[1, :, D // 2 :] = dv


def attend_back(meta, query, key, value, do, turned, lse, bias, mask):
    rows = query.shape[0]
    chunks = rows // CHUNK
    tile = pl.BlockSpec((CHUNK, D), lambda c, m: (c, 0))
    return pl.pallas_call(
        attend_back_kernel,
        grid_spec=pltpu.PrefetchScalarGridSpec(
            num_scalar_prefetch=1,
            grid=(chunks,),
            in_specs=[
                tile, tile, tile, tile,
                pl.BlockSpec((1, D, CHUNK), lambda c, m: (c, 0, 0)),
                pl.BlockSpec((1, 16, CHUNK), lambda c, m: (c, 0, 0)),
                pl.BlockSpec((1, HEADS, CHUNK, CHUNK), lambda c, m: (m[META_KIND + c], 0, 0, 0)),
                pl.BlockSpec((CHUNK, 1), lambda c, m: (c, 0)),
            ],
            out_specs=[
                pl.BlockSpec((2, CHUNK, 3 * D // 2), lambda c, m: (0, c, 0)),
                full(2, HEADS, CHUNK, CHUNK),
            ],
            scratch_shapes=[pltpu.VMEM((D, CHUNK), F32), pltpu.VMEM((D, CHUNK), F32)],
        ),
        out_shape=[
            jax.ShapeDtypeStruct((2, rows, 3 * D // 2), BF16),
            jax.ShapeDtypeStruct((2, HEADS, CHUNK, CHUNK), F32),
        ],
        compiler_params=pltpu.CompilerParams(vmem_limit_bytes=VMEM_BIG),
        cost_estimate=pl.CostEstimate(
            flops=10 * rows * CHUNK * D * 3, bytes_accessed=30 * rows * D, transcendentals=0
        ),
        name="attend_back",
    )(meta, query, key, value, do, turned, lse, bias, mask)


def last_kernel(
    meta, dqkv_ref, x_ref, dx_ref, vec_ref, a0, a1, b0, b1,
    out_ref, sums_ref, sums_p_ref, w_scr, sem,
):
    @pl.when(pl.program_id(0) == 0)
    def _():
        load = Load(meta, sem, w_scr)
        load.cols("a", a0, a1, 0)
        load.cols("b", b0, b1, a0.shape[2])
        load.wait()
        sums_ref[...] = jnp.zeros_like(sums_ref)
        sums_p_ref[...] = jnp.zeros_like(sums_p_ref)

    dh = dot(dqkv_ref[0], w_scr[0], NT) + dot(dqkv_ref[1], w_scr[1], NT)
    for half in range(2):
        sums_p_ref[half : half + 1] += col_sum(dqkv_ref[half].astype(F32))
    scaled, spread = unit_rows(x_ref[...].astype(F32))
    sums_ref[0:1] += col_sum(dh * scaled)
    sums_ref[1:2] += col_sum(dh)
    out_ref[...] = (dx_ref[...] + unit_rows_back(dh * vec_ref[0:1], scaled, spread)).astype(BF16)


def last(meta, dqkv, tokens, dx, vec, w_in):
    rows = tokens.shape[0]
    tile = pl.BlockSpec((CHUNK, D), lambda c, m: (c, 0))
    return pl.pallas_call(
        last_kernel,
        grid_spec=pltpu.PrefetchScalarGridSpec(
            num_scalar_prefetch=1,
            grid=(rows // CHUNK,),
            in_specs=[
                pl.BlockSpec((2, CHUNK, 3 * D // 2), lambda c, m: (0, c, 0)),
                tile, tile,
                full(16, D),
                ANY, ANY, ANY, ANY,
            ],
            out_specs=[tile, full(8, D), full(2, 3 * D // 2)],
            scratch_shapes=[pltpu.VMEM((2, D, 3 * D // 2), BF16), pltpu.SemaphoreType.DMA],
        ),
        out_shape=[
            jax.ShapeDtypeStruct((rows, D), BF16),
            jax.ShapeDtypeStruct((8, D), F32),
            jax.ShapeDtypeStruct((2, 3 * D // 2), F32),
        ],
        compiler_params=pltpu.CompilerParams(vmem_limit_bytes=VMEM_BIG),
        cost_estimate=pl.CostEstimate(
            flops=2 * rows * D * 3 * D, bytes_accessed=16 * rows * D, transcendentals=0
        ),
        name="last",
    )(meta, dqkv, tokens, dx, vec, *w_in)


BAND = 384


def cols_grad_kernel(meta, left_ref, right_ref, *out_refs, parts):
    step = pl.program_id(0)
    band = dot(left_ref[...], right_ref[0], TN).astype(BF16)
    at = 0
    for (order, width), out_ref in zip(parts, out_refs):
        for i in range(BAND // ROWS_D):
            piece = meta[META_TO[order] + step * (BAND // ROWS_D) + i]
            out_ref[piece] = band[i * ROWS_D : (i + 1) * ROWS_D, at : at + width]
        at += width


def cols_grad(meta, left, right, parts, own):
    rows, width = left.shape[0], right.shape[2]
    half = (lambda i, m: (m[0], 0, 0)) if own else (lambda i, m: (1 - m[0], 0, 0))
    return pl.pallas_call(
        functools.partial(cols_grad_kernel, parts=parts),
        grid_spec=pltpu.PrefetchScalarGridSpec(
            num_scalar_prefetch=1,
            grid=(D // BAND,),
            in_specs=[
                pl.BlockSpec((rows, BAND), lambda i, m: (0, i)),
                pl.BlockSpec((1, rows, width), half),
            ],
            out_specs=[full(PIECES, ROWS_D, w) for _, w in parts],
        ),
        out_shape=[jax.ShapeDtypeStruct((PIECES, ROWS_D, w), BF16) for _, w in parts],
        compiler_params=pltpu.CompilerParams(vmem_limit_bytes=VMEM_BIG),
        cost_estimate=pl.CostEstimate(
            flops=2 * rows * D * width, bytes_accessed=2 * rows * (D + width), transcendentals=0
        ),
        name="cols_grad_own" if own else "cols_grad_other",
    )(meta, left, right)


def rows_grad_kernel(meta, left_ref, right_ref, own_ref, other_ref, *, order):
    step = pl.program_id(0)
    band = dot(left_ref[...], right_ref[...], TN).astype(BF16)
    low_core = meta[0] == 0
    for i in range(BAND // (2 * ROWS_F)):
        piece = meta[META_TO[order] + step * (BAND // (2 * ROWS_F)) + i]
        even = band[2 * i * ROWS_F : (2 * i + 1) * ROWS_F]
        odd = band[(2 * i + 1) * ROWS_F : (2 * i + 2) * ROWS_F]
        own_ref[piece] = jnp.where(low_core, even, odd)
        other_ref[piece] = jnp.where(low_core, odd, even)


def rows_grad(meta, left, right, order):
    rows = left.shape[0]
    return pl.pallas_call(
        functools.partial(rows_grad_kernel, order=order),
        grid_spec=pltpu.PrefetchScalarGridSpec(
            num_scalar_prefetch=1,
            grid=(FF // BAND,),
            in_specs=[
                pl.BlockSpec((rows, BAND), lambda i, m: (0, i)),
                pl.BlockSpec((rows, D), lambda i, m: (0, 0)),
            ],
            out_specs=[full(PIECES, ROWS_F, D)] * 2,
        ),
        out_shape=[jax.ShapeDtypeStruct((PIECES, ROWS_F, D), BF16)] * 2,
        compiler_params=pltpu.CompilerParams(vmem_limit_bytes=VMEM_BIG),
        cost_estimate=pl.CostEstimate(
            flops=2 * rows * D * FF, bytes_accessed=2 * rows * (D + FF), transcendentals=0
        ),
        name="rows_grad",
    )(meta, left, right)


def swap(values, mask, count):
    return lax.ppermute(values, AXES, [(i, i ^ mask) for i in range(count)])


class Cube:
    SIDES = {"a": (2, 4), "b": (4, 2)}

    def __init__(self):
        self.me = lax.axis_index(AXES).astype(jnp.int32)

    def swap(self, values, mask):
        return swap(values, mask, 32)

    def masks(self, order):
        shift = self.SIDES[order]
        return np.array(
            [8 * (k & 3) + shift[0] * (k >> 2 & 1) + shift[1] * (k >> 3) for k in range(PIECES)]
        )

    def meta(self):
        chip = self.me >> 1
        place = jnp.arange(PIECES, dtype=jnp.int32)
        start = [chip ^ jnp.asarray(self.masks(o) >> 1, jnp.int32) for o in "ab"]
        mask = chip ^ place
        x, y = mask & 1, mask >> 1 & 1
        to = [(mask >> 2) + 4 * x + 8 * y, (mask >> 2) + 4 * y + 8 * x]
        return self.me & 1, start + to

    def spread(self, piece, order):
        held = jnp.stack([piece] + [self.swap(piece, 8 * z) for z in (1, 2, 3)])
        for side in self.SIDES[order]:
            held = jnp.concatenate([held, self.swap(held, side)])
        return held

    def gather_cols(self, shard, parts):
        half = shard.shape[1] // 2
        left, right = shard[:, :half], shard[:, half:]
        odd = (self.me & 1) == 1
        got = self.swap(jnp.where(odd, left, right), 1)
        mine = jnp.where(odd, right, left)
        block = jnp.where(odd, jnp.concatenate([got, mine]), jnp.concatenate([mine, got]))
        out, at = [], 0
        for order, width in parts:
            own = self.spread(block[:, at : at + width], order)
            out += [own, self.swap(own, 1)]
            at += width
        return out

    def gather_rows(self, shard, order):
        own = self.spread(shard, order)
        return [own, self.swap(own, 1)]

    def gather_small(self, pack):
        held = jnp.stack([pack] + [self.swap(pack, 8 * z) for z in (1, 2, 3)])
        held = jnp.stack([held] + [self.swap(held, s) for s in (2, 4, 6)])
        held = jnp.stack([held, self.swap(held, 1)]).reshape(32, -1)
        k = np.arange(32)
        masks = jnp.asarray(8 * (k & 3) + 2 * (k >> 2 & 3) + (k >> 4), jnp.int32)
        device = jnp.arange(32, dtype=jnp.int32)
        pick = (device[:, None] ^ masks[None, :]) == self.me
        return dot(pick.astype(BF16), held)

    def reduce_pieces(self, own, other, order):
        total = own.astype(F32) + self.swap(other, 1).astype(F32)
        for side in self.SIDES[order][::-1]:
            count = total.shape[0] // 2
            total = total[:count] + self.swap(total[count:].astype(BF16), side).astype(F32)
        out = total[0]
        for z in (1, 2, 3):
            out = out + self.swap(total[z].astype(BF16), 8 * z).astype(F32)
        return out

    def reduce_cols(self, own, other, parts):
        sums = [self.reduce_pieces(*pair, order) for *pair, (order, _) in zip(own, other, parts)]
        block = sums[0] if len(sums) == 1 else jnp.concatenate(sums, axis=1)
        rows = block.shape[0] // 2
        low, high = block[:rows], block[rows:]
        odd = (self.me & 1) == 1
        got = self.swap(jnp.where(odd, low, high), 1)
        mine = jnp.where(odd, high, low)
        return jnp.where(
            odd, jnp.concatenate([got, mine], axis=1), jnp.concatenate([mine, got], axis=1)
        )

    def reduce_rows(self, own, other, order):
        return self.reduce_pieces(own, other, order)

    def reduce_small(self, pack):
        k = np.arange(32)
        masks = jnp.asarray(8 * (k & 3) + 2 * (k >> 2 & 3) + (k >> 4), jnp.int32)
        device = jnp.arange(32, dtype=jnp.int32)
        pick = (device[None, :] ^ masks[:, None]) == self.me
        total = jnp.dot(pick.astype(F32), pack, precision=lax.Precision.HIGHEST)
        total = total[:16] + self.swap(total[16:], 1)
        total = total[:4] + sum(self.swap(total[4 * s : 4 * s + 4], 2 * s) for s in (1, 2, 3))
        return total[0] + sum(self.swap(total[z], 8 * z) for z in (1, 2, 3))


class Plain:
    def __init__(self, count):
        self.count = count
        self.me = lax.axis_index(AXES)

    def meta(self):
        place = jnp.arange(PIECES, dtype=jnp.int32)
        return jnp.int32(0), [place] * 4

    def gather_cols(self, shard, parts):
        whole = lax.all_gather(shard, AXES, axis=0, tiled=True)
        out, at, half = [], 0, shard.shape[1] // 2
        for _, width in parts:
            for start in (at, at + half):
                out.append(whole[:, start : start + width].reshape(PIECES, -1, width))
            at += width
        return out

    def gather_rows(self, shard, order):
        whole = lax.all_gather(shard, AXES, axis=0, tiled=True)
        whole = whole.reshape(PIECES, 2, -1, whole.shape[1])
        return [whole[:, 0], whole[:, 1]]

    def gather_small(self, pack):
        return lax.all_gather(pack, AXES).reshape(self.count, -1).astype(F32)

    def reduce_cols(self, own, other, parts):
        whole = jnp.concatenate([p.reshape(-1, p.shape[2]) for p in (*own, *other)], axis=1)
        return lax.psum_scatter(whole.astype(F32), AXES, scatter_dimension=0, tiled=True)

    def reduce_rows(self, own, other, order):
        whole = jnp.stack([own, other], axis=1).reshape(-1, own.shape[2])
        return lax.psum_scatter(whole.astype(F32), AXES, scatter_dimension=0, tiled=True)

    def reduce_small(self, pack):
        return lax.psum_scatter(pack, AXES, scatter_dimension=0, tiled=False)


PARTS_IN = (("a", 640), ("b", 512))
PARTS_OUT = (("a", D // 2),)
PARTS_FF = (("a", FF // 2),)


def layout(bucket, lengths, row_count):
    large = jnp.sum((bucket == 1).astype(jnp.int32), dtype=jnp.int32)
    place = jnp.arange(row_count, dtype=jnp.int32)
    is_large = place < large * SLOT_L
    slot = jnp.where(is_large, place // SLOT_L, large + (place - large * SLOT_L) // SLOT_S)
    offset = jnp.where(is_large, place % SLOT_L, place % SLOT_S)
    picked = slot[:, None] == jnp.arange(bucket.shape[0], dtype=jnp.int32)[None, :]
    live_count = jnp.sum(jnp.where(picked, lengths[None, :], 0), axis=1, dtype=jnp.int32)
    live = (offset < live_count).astype(F32)[:, None]
    chunk = jnp.arange(row_count // CHUNK, dtype=jnp.int32)
    return live, (chunk >= large).astype(jnp.int32)


def body(
    tokens,
    cotangent,
    w_attn_in,
    w_attn_out,
    w_fc_in,
    w_fc_out,
    gains_d,
    biases_d,
    gains_ff,
    biases_ff,
    rel_table,
    head_scale,
    bucket,
    lengths,
    *,
    count,
    cube,
):
    net = Cube() if cube else Plain(count)
    rows = tokens.shape[0]

    small = (gains_d, biases_d, gains_ff[None], biases_ff, rel_table)
    sizes = [v.size for v in small]
    ends = np.cumsum(sizes)
    width = -(-int(ends[-1] + HEADS) // 1024) * 1024
    pack = jnp.concatenate([v.reshape(-1) for v in small] + [jnp.zeros(width - ends[-1], BF16)])
    whole = net.gather_small(pack)
    gain_rows, bias_rows, gain_mid, bias_mid, table = (
        whole[:, end - size : end]
        .reshape(count, v.shape[0], v.shape[1])
        .transpose(1, 0, 2)
        .reshape(v.shape[0], -1)
        for v, size, end in zip(small, sizes, ends)
    )
    in_pieces = net.gather_cols(w_attn_in, PARTS_IN)
    out_pieces = net.gather_cols(w_attn_out, PARTS_OUT)
    ff_pieces = net.gather_cols(w_fc_in, PARTS_FF)
    down_pieces = net.gather_rows(w_fc_out, "b")

    head_wide = jnp.repeat(head_scale.astype(F32), HEAD_DIM)[None]
    vec = jnp.concatenate([gain_rows, bias_rows, head_wide, jnp.zeros((5, D), F32)])
    wide = jnp.concatenate([gain_mid, bias_mid, jnp.zeros((5, FF), F32)])
    live, kinds = layout(bucket, lengths, rows)
    mask = (1.0 - live) * NEG_FILL
    core, tables = net.meta()
    meta = jnp.concatenate(
        [core.astype(jnp.int32)[None], kinds, jnp.zeros(7 - kinds.shape[0], jnp.int32), *tables]
    )
    keys, keys_back, queries = (jnp.asarray(t) for t in pick_tables())
    flipped = jnp.pad(table[:, 1006::-1], ((0, 0), (0, RELS - 1007)))[:, None]
    bias = build_bias(flipped, keys, queries)

    low_in, query, key, value, mixed, turned, lse = attend(
        meta, tokens, vec, in_pieces, bias, mask
    )
    out_tokens, mid, low_attn, low_mid, low_ff, dz, df, sums_a, sums_ff = feed(
        meta, tokens, mixed, cotangent, live, vec, wide, out_pieces, ff_pieces, down_pieces
    )
    own, other = rows_grad(meta, low_ff, df, "b")
    grad_fc_out = net.reduce_rows(own, other, "b")

    da, dx, do, sums_b = middle(
        meta, dz, mid, mixed, cotangent, live, vec, ff_pieces, out_pieces
    )
    other, own = (cols_grad(meta, low_mid, dz, PARTS_FF, side) for side in (False, True))
    grad_fc_in = net.reduce_cols(own, other, PARTS_FF)
    other, own = (cols_grad(meta, low_attn, da, PARTS_OUT, side) for side in (False, True))
    grad_attn_out = net.reduce_cols(own, other, PARTS_OUT)

    dqkv, tiles = attend_back(meta, query, key, value, do, turned, lse, bias, mask)
    other, own = (cols_grad(meta, low_in, dqkv, PARTS_IN, side) for side in (False, True))
    grad_attn_in = net.reduce_cols(own, other, PARTS_IN)
    grad_table = table_grads(tiles, keys_back, queries)
    grad_tokens, sums_c, sums_p = last(meta, dqkv, tokens, dx, vec, in_pieces)

    sums_p = sums_p.reshape(3, D)
    d_terms = jnp.concatenate(
        [
            sums_c[0:1], sums_b[3:4], sums_b[0:1],
            sums_c[1:2], sums_p[0:1], sums_p[2:3], sums_b[4:5], sums_b[2:3], sums_b[1:2], sums_a[0:1],
        ]
    )
    head_terms = jnp.sum(sums_b[5].reshape(HEADS, HEAD_DIM), axis=1)
    terms = (d_terms[:3], d_terms[3:], sums_ff[0:1], sums_ff[2:0:-1], grad_table)
    terms = [
        t.reshape(t.shape[0], count, -1).transpose(1, 0, 2).reshape(count, -1) for t in terms
    ]
    terms += [jnp.broadcast_to(head_terms, (count, HEADS)), jnp.zeros((count, width - ends[-1] - HEADS), F32)]
    mine = net.reduce_small(jnp.concatenate(terms, axis=1))
    grads = [
        mine[end - size : end].reshape(v.shape) for v, size, end in zip(small, sizes, ends)
    ]
    grad_head_scale = mine[ends[-1] : ends[-1] + HEADS]
    return (
        out_tokens,
        grad_tokens,
        grad_attn_in,
        grad_attn_out,
        grad_fc_in,
        grad_fc_out,
        grads[0],
        grads[1],
        grads[2][0],
        grads[3],
        grads[4],
        grad_head_scale,
    )


def solution(mesh):
    rows = P(AXES, None)
    columns = P(None, AXES)
    line = P(AXES)
    count = mesh.shape["wide"] * mesh.shape["narrow"]
    cube = (mesh.shape["wide"], mesh.shape["narrow"]) == (8, 4)
    return jax.shard_map(
        functools.partial(body, count=count, cube=cube),
        mesh=mesh,
        in_specs=(
            rows, rows, rows, rows, rows, rows,
            columns, columns, line, columns, columns, P(), line, line,
        ),
        out_specs=(
            rows, rows, rows, rows, rows, rows,
            columns, columns, line, columns, columns, P(),
        ),
        check_vma=False,
    )
```

time: 1400 us -> 498 us (0.36)
  waiting for transfers between devices: 518 us -> 133 us
  matrix products: 301 us -> 0.4 us
  blocking collectives: 236 us -> 0 us
  Pallas kernels: 0 us -> 207 us
  local copies, waits for them, and re-layouts: 234 us -> 39.3 us
  starting transfers between devices: 0.4 us -> 85.2 us
  other arithmetic: 76.1 us -> 23.3 us
    reduce_scatter x4 -> x0, waiting for transfers between devices: 508 us -> none  [the longest x1 142 us: body(): lax.psum_scatter(grad_fc_in, ('wide', 'narrow'), scatter_dimension=0, til...]
    dot_general x42 -> x2, matrix products: 301 us -> 0.4 us  [the longest x1 0.25 us: reduce_small(): total = jnp.dot(pick.astype(F32), pack, precision=lax.Precision.HIGHEST)]
    pallas_call x0 -> x14, Pallas kernels: none -> 207 us  [the longest x1 57.1 us: feed(): pl.pallas_call(feed_kernel, grid_spec=pltpu.PrefetchScalarGridSpec(num_sc...]
    all_gather x4 -> x0, blocking collectives: 156 us -> none  [the longest x1 43.8 us: body(): lax.all_gather(biases_d, ('wide', 'narrow'), axis=1, tiled=True)]
    ppermute x0 -> x80, waiting for transfers between devices: none -> 133 us  [swap(): return lax.ppermute(values, AXES, [(i, i ^ mask) for i in range(count)])]
    gather x3 -> x0, local copies, waits for them, and re-layouts: 114 us -> none  [pair_bias(): return jnp.take(bias_table, pair_index, axis=1)]
    ppermute x0 -> x80, starting transfers between devices: none -> 85.2 us  [swap(): return lax.ppermute(values, AXES, [(i, i ^ mask) for i in range(count)])]
    unnamed x2 -> x0, blocking collectives: 80.5 us -> none
  transfers between devices with their start and end apart: 10 -> 80, of which waited for: 5 -> 36; matrix products, arithmetic and copies ran while one was open for 38% -> 10% of each run, Pallas kernels for 0% -> 14%
where the time goes in v1:
time: 498 us; the launch traced here: 491 us
  Pallas kernels  207 us (42%)
  waiting for transfers between devices  133 us (27%)
  starting transfers between devices  85.2 us (17%)
  local copies, waits for them, and re-layouts  39.3 us (8%)
  other arithmetic  23.3 us (5%)
    ppermute x80, waiting for transfers between devices, swap(): return lax.ppermute(values, AXES, [(i, i ^ mask) for i in range(count)])  133 us
    ppermute x80, starting transfers between devices, swap(): return lax.ppermute(values, AXES, [(i, i ^ mask) for i in range(count)])  85.2 us
    pallas_call x1, Pallas kernels, feed(): pl.pallas_call(feed_kernel, grid_spec=pltpu.PrefetchScalarGridSpec(num_sc...  57.1 us
    pallas_call x6, Pallas kernels, cols_grad(): pl.pallas_call(functools.partial(cols_grad_kernel, parts=parts), grid_spe...  34.3 us
    pallas_call x1, Pallas kernels, attend(): pl.pallas_call(attend_kernel, grid_spec=pltpu.PrefetchScalarGridSpec(num_...  24.6 us
    pallas_call x1, Pallas kernels, middle(): pl.pallas_call(middle_kernel, grid_spec=pltpu.PrefetchScalarGridSpec(num_...  20.3 us
    pallas_call x1, Pallas kernels, attend_back(): pl.pallas_call(attend_back_kernel, grid_spec=pltpu.PrefetchScalarGridSpec...  19 us
    pallas_call x1, Pallas kernels, table_grads(): pl.pallas_call(table_kernel, grid=(HEADS,), in_specs=[pl.BlockSpec((2, 1,...  15.4 us
  transfers between devices with their start and end apart: 80, of which 36 were waited for; matrix products, arithmetic and copies ran while one was open for 10% of the time, Pallas kernels for 14%

profile of v1, /device:TPU:0, one launch (start us, length us, event | category | flops | bytes accessed | tf_op | source)
XLA Modules:
  0.0 491.1 jit_solution(5669689799927141056)
XLA Ops:
  4.5 3.0 collective-permute-start
  11.1 3.5 collective-permute-start.35
  36.5 3.9 collective-permute-done.21
  41.0 4.2 collective-permute-done.22
  46.1 5.0 %collective-permute-done.23 = bf16[48,384]{1,0:T(8,128)(2,1)S(1)} collective-permute-done((bf16[48,384]{1,0:T(8,128)(2,1)S(1)}, bf16[48,384]{1,0:T(8,128)(2,1)S(1)}, u32[]{:S(2)}, u32[]{:S(2)}) %collective-permute-start.23) | collective-permute-done | bytes 36896 | tf_op jit(solution)/shard_map/ppermute | solution.py:669
  63.6 2.9 collective-permute-done.28
  66.5 3.0 collective-permute-done.29
  73.3 7.2 %collective-permute-done.37 = bf16[4,96,768]{2,1,0:T(8,128)(2,1)S(1)} collective-permute-done((bf16[4,96,768]{2,1,0:T(8,128)(2,1)S(1)}, bf16[4,96,768]{2,1,0:T(8,128)(2,1)S(1)}, u32[]{:S(2)}, u32[]{:S(2)}) %collective-permute-start.37) | collective-permute-done | bytes 589856 | tf_op jit(solution)/shard_map/ppermute | solution.py:669
  94.1 15.5 %collective-permute-done.38 = bf16[8,96,768]{2,1,0:T(8,128)(2,1)S(1)} collective-permute-done((bf16[8,96,768]{2,1,0:T(8,128)(2,1)S(1)}, bf16[8,96,768]{2,1,0:T(8,128)(2,1)S(1)}, u32[]{:S(2)}, u32[]{:S(2)}) %collective-permute-start.38) | collective-permute-done | bytes 1179680 | tf_op jit(solution)/shard_map/ppermute | solution.py:669
  118.4 13.5 %collective-permute-done.25 = bf16[8,48,384]{2,1,0:T(8,128)(2,1)S(1)} collective-permute-done((bf16[8,48,384]{2,1,0:T(8,128)(2,1)S(1)}, bf16[8,48,384]{2,1,0:T(8,128)(2,1)S(1)}, u32[]{:S(2)}, u32[]{:S(2)}) %collective-permute-start.25) | collective-permute-done | bytes 294944 | tf_op jit(solution)/shard_map/ppermute | solution.py:669
  138.1 12.4 %bias_tiles.1.bias_ref = bf16[2,12,256,256]{3,2,1,0:T(8,128)(2,1)} custom-call(f32[12,1,1024]{2,1,0:T(1,128)} %broadcast_in_dim.48.table_ref, bf16[2,256,512]{2,1,0:T(8,128)(2,1)} %constant.98.clone.keys_ref, bf16[2,256,256]{2,1,0:T(8,128)(2,1)} %constant.100.clone.queries_ref), custom_call_target="tpu_custom_call" | custom-call | tf_op jit(solution)/shard_map/bias_tiles/pallas_call | solution.py:102
  152.2 24.6 %attend.1 = (bf16[1024,768]{1,0:T(8,128)(2,1)}, bf16[1024,768]{1,0:T(8,128)(2,1)}, bf16[1024,768]{1,0:T(8,128)(2,1)}, bf16[1024,768]{1,0:T(8,128)(2,1)}, f32[102...) custom-call(s32[72]{0:T(128)} %concatenate.145.meta, bf16[1024,768]{1,0:T(8,128)(2,1)} %x_ref.5, ...), custom_call_target="tpu_custom_call" | custom-call | flops 3623878656 | bytes 18874368 | tf_op jit(solution)/shard_map/attend/pallas_call | solution.py:236
  177.6 57.1 %feed.1 = (bf16[1024,768]{1,0:T(8,128)(2,1)}, f32[1024,768]{1,0:T(8,128)}, bf16[1024,768]{1,0:T(8,128)(2,1)}, bf16[1024,768]{1,0:T(8,128)(2,1)}, bf16[1024,3072]...) custom-call(s32[72]{0:T(128)} %concatenate.145.meta, ...), custom_call_target="tpu_custom_call" | custom-call | flops 15703474176 | bytes 31457280 | tf_op jit(solution)/shard_map/feed/pallas_call | solution.py:349
  236.4 7.1 %cols_grad_own.5 = bf16[16,48,1536]{2,1,0:T(8,128)(2,1)} custom-call(s32[72]{0:T(128)} %concatenate.145.meta, bf16[1024,768]{1,0:T(8,128)(2,1)} %get-tuple-element.63.left_ref, bf16[2,1024,1536]{2,1,0:T(8,128)(2,1)} %get-tuple-element.48.dz_ref.right_ref), custom_call_target="tpu_custom_call" | custom-call | flops 2415919104 | bytes 4718592 | tf_op jit(solution)/shard_map/cols_grad_own/pallas_call | solution.py:614
  243.5 7.1 %cols_grad_other.5 = bf16[16,48,1536]{2,1,0:T(8,128)(2,1)} custom-call(s32[72]{0:T(128)} %concatenate.145.meta, bf16[1024,768]{1,0:T(8,128)(2,1)} %get-tuple-element.63.left_ref, bf16[2,1024,1536]{2,1,0:T(8,128)(2,1)} %get-tuple-element.48.dz_ref.right_ref), custom_call_target="tpu_custom_call" | custom-call | flops 2415919104 | bytes 4718592 | tf_op jit(solution)/shard_map/cols_grad_other/pallas_call | solution.py:614
  250.6 20.3 %middle.1 = (bf16[2,1024,384]{2,1,0:T(8,128)(2,1)}, f32[1024,768]{1,0:T(8,128)}, bf16[1024,768]{1,0:T(8,128)(2,1)}, f32[8,768]{1,0:T(8,128)}) custom-call(s32[72]{0:T(128)} %concatenate.145.meta, bf16[2,1024,1536]{2,1,0:T(8,128)(2,1)} %get-tuple-element.48.dz_ref.right_ref, f32[1024,768]{1,0:T(8,128)} %get-tuple-element.49.mid_ref, ...), custom_call_target="tpu_custom_call" | custom-call | flops 6039797760 | bytes 23592960 | tf_op jit(solution)/shard_map/middle/pallas_call | solution.py:435
  270.9 19.0 %attend_back.1 = (bf16[2,1024,1152]{2,1,0:T(8,128)(2,1)}, f32[2,12,256,256]{3,2,1,0:T(8,128)}) custom-call(s32[72]{0:T(128)} %concatenate.145.meta, bf16[1024,768]{1,0:T(8,128)(2,1)} %get-tuple-element.45.q_ref, bf16[1024,768]{1,0:T(8,128)(2,1)} %get-tuple-element.46.k_ref, bf16[1024,768]{1,0:T(8,128)(2,1)} %get-tuple-element.47.v_ref, ...), custom_call_target="tpu_custom_call" | custom-call | flops 6039797760 | bytes 23592960 | tf_op jit(solution)/shard_map/attend_back/pallas_call | solution.py:515
  289.9 11.3 %last.1 = (bf16[1024,768]{1,0:T(8,128)(2,1)}, f32[8,768]{1,0:T(8,128)}, f32[2,1152]{1,0:T(2,128)}) custom-call(s32[72]{0:T(128)} %concatenate.145.meta, bf16[2,1024,1152]{2,1,0:T(8,128)(2,1)} %get-tuple-element.53.dqkv_ref.right_ref, bf16[1024,768]{1,0:T(8,128)(2,1)} %x_ref.5, f32[1024,768]{1,0:T(8,128)} %get-tuple-element.54.dx_ref, ...), custom_call_target="tpu_custom_call" | custom-call | flops 3623878656 | bytes 12582912 | tf_op jit(solution)/shard_map/last/pallas_call | solution.py:570
  304.2 15.4 %table_grads.1 = f32[12,8,1024]{2,1,0:T(8,128)} custom-call(f32[2,12,256,256]{3,2,1,0:T(8,128)} %get-tuple-element.73.tiles_ref, bf16[2,256,512]{2,1,0:T(8,128)(2,1)} %constant.99.clone.keys_ref, bf16[2,256,256]{2,1,0:T(8,128)(2,1)} %constant.100.clone.queries_ref), custom_call_target="tpu_custom_call" | custom-call | tf_op jit(solution)/shard_map/table_grads/pallas_call | solution.py:138
  323.1 4.1 cols_grad_other.4
  327.2 6.0 %cols_grad_other.3 = (bf16[16,48,640]{2,1,0:T(8,128)(2,1)}, bf16[16,48,512]{2,1,0:T(8,128)(2,1)}) custom-call(s32[72]{0:T(128)} %concatenate.145.meta, bf16[1024,768]{1,0:T(8,128)(2,1)} %get-tuple-element.56.left_ref, bf16[2,1024,1152]{2,1,0:T(8,128)(2,1)} %get-tuple-element.53.dqkv_ref.right_ref), custom_call_target="tpu_custom_call" | custom-call | flops 1811939328 | bytes 3932160 | tf_op jit(solution)/shard_map/cols_grad_other/pallas_call | solution.py:614
  333.7 12.5 %rows_grad.1 = (bf16[16,96,768]{2,1,0:T(8,128)(2,1)}, bf16[16,96,768]{2,1,0:T(8,128)(2,1)}) custom-call(s32[72]{0:T(128)} %concatenate.145.meta, bf16[1024,3072]{1,0:T(8,128)(2,1)} %get-tuple-element.64.left_ref, bf16[1024,768]{1,0:T(8,128)(2,1)} %get-tuple-element.65.right_ref), custom_call_target="tpu_custom_call" | custom-call | flops 4831838208 | bytes 7864320 | tf_op jit(solution)/shard_map/rows_grad/pallas_call | solution.py:648
  346.2 6.0 %cols_grad_own.3 = (bf16[16,48,640]{2,1,0:T(8,128)(2,1)}, bf16[16,48,512]{2,1,0:T(8,128)(2,1)}) custom-call(s32[72]{0:T(128)} %concatenate.145.meta, bf16[1024,768]{1,0:T(8,128)(2,1)} %get-tuple-element.56.left_ref, bf16[2,1024,1152]{2,1,0:T(8,128)(2,1)} %get-tuple-element.53.dqkv_ref.right_ref), custom_call_target="tpu_custom_call" | custom-call | flops 1811939328 | bytes 3932160 | tf_op jit(solution)/shard_map/cols_grad_own/pallas_call | solution.py:614
  352.2 4.1 cols_grad_own.4
  363.1 4.8 collective-permute-start.77
  376.0 6.4 %collective-permute-start.56 = (bf16[48,384]{1,0:T(8,128)(2,1)S(1)}, bf16[48,384]{1,0:T(8,128)(2,1)S(1)}, u32[]{:S(2)}, u32[]{:S(2)}) collective-permute-start(bf16[48,384]{1,0:T(8,128)(2,1)S(1)} %get-tuple-element.114), channel_id=1, source_target_pairs={{0,8},{1,9},{2,10},{3,11},{4,12},{5,13},{6,14},{7,15},{8,0},{9,1},... | collective-permute-start | bytes 110600 | tf_op jit(solution)/shard_map/ppermute | solution.py:669
  399.9 5.0 %collective-permute-done.41 = bf16[8,48,640]{2,1,0:T(8,128)(2,1)} collective-permute-done((bf16[8,48,640]{2,1,0:T(8,128)(2,1)}, bf16[8,48,640]{2,1,0:T(8,128)(2,1)}, u32[]{:S(2)}, u32[]{:S(2)}) %collective-permute-start.41) | collective-permute-done | bytes 491552 | tf_op jit(solution)/shard_map/ppermute | solution.py:669
  431.0 12.5 %collective-permute-done.61 = bf16[8,48,1536]{2,1,0:T(8,128)(2,1)S(1)} collective-permute-done((bf16[8,48,1536]{2,1,0:T(8,128)(2,1)S(1)}, bf16[8,48,1536]{2,1,0:T(8,128)(2,1)S(1)}, u32[]{:S(2)}, u32[]{:S(2)}) %collective-permute-start.61) | collective-permute-done | bytes 1179680 | tf_op jit(solution)/shard_map/ppermute | solution.py:669
  446.2 12.3 %collective-permute-done.68 = bf16[8,96,768]{2,1,0:T(8,128)(2,1)S(1)} collective-permute-done((bf16[8,96,768]{2,1,0:T(8,128)(2,1)S(1)}, bf16[8,96,768]{2,1,0:T(8,128)(2,1)S(1)}, u32[]{:S(2)}, u32[]{:S(2)}) %collective-permute-start.68) | collective-permute-done | bytes 1179680 | tf_op jit(solution)/shard_map/ppermute | solution.py:669
  460.1 6.1 %collective-permute-done.62 = bf16[4,48,1536]{2,1,0:T(8,128)(2,1)S(1)} collective-permute-done((bf16[4,48,1536]{2,1,0:T(8,128)(2,1)S(1)}, bf16[4,48,1536]{2,1,0:T(8,128)(2,1)S(1)}, u32[]{:S(2)}, u32[]{:S(2)}) %collective-permute-start.62) | collective-permute-done | bytes 589856 | tf_op jit(solution)/shard_map/ppermute | solution.py:669
  476.5 4.2 collective-permute-done.64
  480.9 8.3 %collective-permute-done.71 = bf16[96,768]{1,0:T(8,128)(2,1)S(1)} collective-permute-done((bf16[96,768]{1,0:T(8,128)(2,1)S(1)}, bf16[96,768]{1,0:T(8,128)(2,1)S(1)}, u32[]{:S(2)}, u32[]{:S(2)}) %collective-permute-start.71) | collective-permute-done | bytes 147488 | tf_op jit(solution)/shard_map/ppermute | solution.py:669
  (360 shorter events, 160.2 us)
Async XLA Ops:
  4.5 20.5 %collective-permute-start = (bf16[1024]{0:T(1024)(128)(2,1)S(1)}, bf16[1024]{0:T(1024)(128)(2,1)S(1)}, u32[]{:S(2)}, u32[]{:S(2)}) collective-permute-start(bf16[1024]{0:T(1024)(128)(2,1)S(1)} %concatenate.146), channel_id=1, source_target_pairs={{0,8},{1,9},{2,10},{3,11},{4,12},{5,13},{6,14},{7,15},{8,0},{9,1},... | collective-permute-start | bytes 6152 | tf_op jit(solution)/shard_map/ppermute | solution.py:669
  7.6 17.5 %collective-permute-start.1 = (bf16[1024]{0:T(1024)(128)(2,1)S(1)}, bf16[1024]{0:T(1024)(128)(2,1)S(1)}, u32[]{:S(2)}, u32[]{:S(2)}) collective-permute-start(bf16[1024]{0:T(1024)(128)(2,1)S(1)} %concatenate.146), channel_id=1, source_target_pairs={{0,16},{1,17},{2,18},{3,19},{4,20},{5,21},{6,22},{7,23},{8,24},{9,... | collective-permute-start | bytes 6152 | tf_op jit(solution)/shard_map/ppermute | solution.py:669
  10.2 46.9 %collective-permute-start.34 = (bf16[96,768]{1,0:T(8,128)(2,1)}, bf16[96,768]{1,0:T(8,128)(2,1)S(1)}, u32[]{:S(2)}, u32[]{:S(2)}) collective-permute-start(bf16[96,768]{1,0:T(8,128)(2,1)} %param.26), channel_id=1, source_target_pairs={{0,8},{1,9},{2,10},{3,11},{4,12},{5,13},{6,14},{7,15},{8,0},{9,1},... | collective-permute-start | bytes 442376 | tf_op jit(solution)/shard_map/ppermute | solution.py:669
  11.1 46.7 %collective-permute-start.35 = (bf16[96,768]{1,0:T(8,128)(2,1)}, bf16[96,768]{1,0:T(8,128)(2,1)S(1)}, u32[]{:S(2)}, u32[]{:S(2)}) collective-permute-start(bf16[96,768]{1,0:T(8,128)(2,1)} %param.26), channel_id=1, source_target_pairs={{0,16},{1,17},{2,18},{3,19},{4,20},{5,21},{6,22},{7,23},{8,24},{9,... | collective-permute-start | bytes 442376 | tf_op jit(solution)/shard_map/ppermute | solution.py:669
  28.9 32.1 %collective-permute-start.36 = (bf16[96,768]{1,0:T(8,128)(2,1)S(1)}, bf16[96,768]{1,0:T(8,128)(2,1)S(1)}, u32[]{:S(2)}, u32[]{:S(2)}) collective-permute-start(bf16[96,768]{1,0:T(8,128)(2,1)S(1)} %copy-done.4), channel_id=1, source_target_pairs={{0,24},{1,25},{2,26},{3,27},{4,28},{5,29},{6,30},{7,31},{8,16},{9,... | collective-permute-start | bytes 442376 | tf_op jit(solution)/shard_map/ppermute | solution.py:669
  30.4 21.4 %collective-permute-start.27 = (bf16[24,1536]{1,0:T(8,128)(2,1)S(1)}, bf16[24,1536]{1,0:T(8,128)(2,1)S(1)}, u32[]{:S(2)}, u32[]{:S(2)}) collective-permute-start(bf16[24,1536]{1,0:T(8,128)(2,1)S(1)} %get-tuple-element.132), channel_id=1, source_target_pairs={{0,1},{1,0},{2,3},{3,2},{4,5},{5,4},{6,7},{7,6},{8,9},{9,8},{10,11... | collective-permute-start | bytes 221192 | tf_op jit(solution)/shard_map/ppermute | solution.py:669
  51.8 33.8 %collective-permute-start.15 = (bf16[48,512]{1,0:T(8,128)(2,1)S(1)}, bf16[48,512]{1,0:T(8,128)(2,1)S(1)}, u32[]{:S(2)}, u32[]{:S(2)}) collective-permute-start(bf16[48,512]{1,0:T(8,128)(2,1)S(1)} %get-tuple-element.138), channel_id=1, source_target_pairs={{0,16},{1,17},{2,18},{3,19},{4,20},{5,21},{6,22},{7,23},{8,24},{9,... | collective-permute-start | bytes 147464 | tf_op jit(solution)/shard_map/ppermute | solution.py:669
  55.2 31.1 %collective-permute-start.16 = (bf16[48,512]{1,0:T(8,128)(2,1)S(1)}, bf16[48,512]{1,0:T(8,128)(2,1)S(1)}, u32[]{:S(2)}, u32[]{:S(2)}) collective-permute-start(bf16[48,512]{1,0:T(8,128)(2,1)S(1)} %get-tuple-element.138), channel_id=1, source_target_pairs={{0,24},{1,25},{2,26},{3,27},{4,28},{5,29},{6,30},{7,31},{8,16},{9,... | collective-permute-start | bytes 147464 | tf_op jit(solution)/shard_map/ppermute | solution.py:669
  66.5 21.6 %collective-permute-start.8 = (bf16[48,640]{1,0:T(8,128)(2,1)S(1)}, bf16[48,640]{1,0:T(8,128)(2,1)S(1)}, u32[]{:S(2)}, u32[]{:S(2)}) collective-permute-start(bf16[48,640]{1,0:T(8,128)(2,1)S(1)} %get-tuple-element.142), channel_id=1, source_target_pairs={{0,8},{1,9},{2,10},{3,11},{4,12},{5,13},{6,14},{7,15},{8,0},{9,1},... | collective-permute-start | bytes 184328 | tf_op jit(solution)/shard_map/ppermute | solution.py:669
  83.2 26.3 %collective-permute-start.38 = (bf16[8,96,768]{2,1,0:T(8,128)(2,1)S(1)}, bf16[8,96,768]{2,1,0:T(8,128)(2,1)S(1)}, u32[]{:S(2)}, u32[]{:S(2)}) collective-permute-start(bf16[8,96,768]{2,1,0:T(8,128)(2,1)S(1)} %get-tuple-element.96), channel_id=1, source_target_pairs={{0,2},{1,3},{2,0},{3,1},{4,6},{5,7},{6,4},{7,5},{8,10},{9,11},{10,... | collective-permute-start | bytes 3538952 | tf_op jit(solution)/shard_map/ppermute | solution.py:669
  85.6 25.1 %collective-permute-start.32 = (bf16[8,48,1536]{2,1,0:T(8,128)(2,1)S(1)}, bf16[8,48,1536]{2,1,0:T(8,128)(2,1)S(1)}, u32[]{:S(2)}, u32[]{:S(2)}) collective-permute-start(bf16[8,48,1536]{2,1,0:T(8,128)(2,1)S(1)} %get-tuple-element.98), channel_id=1, source_target_pairs={{0,4},{1,5},{2,6},{3,7},{4,0},{5,1},{6,2},{7,3},{8,12},{9,13},{10,... | collective-permute-start | bytes 3538952 | tf_op jit(solution)/shard_map/ppermute | solution.py:669
  88.1 27.3 %collective-permute-start.24 = (bf16[4,48,384]{2,1,0:T(8,128)(2,1)S(1)}, bf16[4,48,384]{2,1,0:T(8,128)(2,1)S(1)}, u32[]{:S(2)}, u32[]{:S(2)}) collective-permute-start(bf16[4,48,384]{2,1,0:T(8,128)(2,1)S(1)} %pad_maximum_fusion.4), channel_id=1, source_target_pairs={{0,2},{1,3},{2,0},{3,1},{4,6},{5,7},{6,4},{7,5},{8,10},{9,11},{10,... | collective-permute-start | bytes 442376 | tf_op jit(solution)/shard_map/ppermute | solution.py:669
  90.2 26.4 %collective-permute-start.17 = (bf16[4,48,512]{2,1,0:T(8,128)(2,1)S(1)}, bf16[4,48,512]{2,1,0:T(8,128)(2,1)S(1)}, u32[]{:S(2)}, u32[]{:S(2)}) collective-permute-start(bf16[4,48,512]{2,1,0:T(8,128)(2,1)S(1)} %pad_maximum_fusion.3), channel_id=1, source_target_pairs={{0,4},{1,5},{2,6},{3,7},{4,0},{5,1},{6,2},{7,3},{8,12},{9,13},{10,... | collective-permute-start | bytes 589832 | tf_op jit(solution)/shard_map/ppermute | solution.py:669
  92.5 21.2 %collective-permute-start.11 = (bf16[4,48,640]{2,1,0:T(8,128)(2,1)S(1)}, bf16[4,48,640]{2,1,0:T(8,128)(2,1)S(1)}, u32[]{:S(2)}, u32[]{:S(2)}) collective-permute-start(bf16[4,48,640]{2,1,0:T(8,128)(2,1)S(1)} %pad_maximum_fusion.2), channel_id=1, source_target_pairs={{0,2},{1,3},{2,0},{3,1},{4,6},{5,7},{6,4},{7,5},{8,10},{9,11},{10,... | collective-permute-start | bytes 737288 | tf_op jit(solution)/shard_map/ppermute | solution.py:669
  110.7 66.2 %collective-permute-start.39 = (bf16[16,96,768]{2,1,0:T(8,128)(2,1)}, bf16[16,96,768]{2,1,0:T(8,128)(2,1)}, u32[]{:S(2)}, u32[]{:S(2)}) collective-permute-start(bf16[16,96,768]{2,1,0:T(8,128)(2,1)} %constant_dynamic-update-slice_fusion.49.f0), channel_id=1, source_target_pairs={{0,1},{1,0},{2,3},{3,2},{4,5},{5,4},{6,7},{7,6},{8,9},{9,8},{10,11... | collective-permute-start | bytes 7077896 | tf_op jit(solution)/shard_map/ppermute | solution.py:669
  111.8 65.0 %collective-permute-start.33 = (bf16[16,48,1536]{2,1,0:T(8,128)(2,1)}, bf16[16,48,1536]{2,1,0:T(8,128)(2,1)}, u32[]{:S(2)}, u32[]{:S(2)}) collective-permute-start(bf16[16,48,1536]{2,1,0:T(8,128)(2,1)} %constant_dynamic-update-slice_fusion.38.i0), channel_id=1, source_target_pairs={{0,1},{1,0},{2,3},{3,2},{4,5},{5,4},{6,7},{7,6},{8,9},{9,8},{10,11... | collective-permute-start | bytes 7077896 | tf_op jit(solution)/shard_map/ppermute | solution.py:669
  113.8 18.9 %collective-permute-start.12 = (bf16[8,48,640]{2,1,0:T(8,128)(2,1)S(1)}, bf16[8,48,640]{2,1,0:T(8,128)(2,1)S(1)}, u32[]{:S(2)}, u32[]{:S(2)}) collective-permute-start(bf16[8,48,640]{2,1,0:T(8,128)(2,1)S(1)} %get-tuple-element.105), channel_id=1, source_target_pairs={{0,4},{1,5},{2,6},{3,7},{4,0},{5,1},{6,2},{7,3},{8,12},{9,13},{10,... | collective-permute-start | bytes 1474568 | tf_op jit(solution)/shard_map/ppermute | solution.py:669
  116.7 17.4 %collective-permute-start.18 = (bf16[8,48,512]{2,1,0:T(8,128)(2,1)S(1)}, bf16[8,48,512]{2,1,0:T(8,128)(2,1)S(1)}, u32[]{:S(2)}, u32[]{:S(2)}) collective-permute-start(bf16[8,48,512]{2,1,0:T(8,128)(2,1)S(1)} %get-tuple-element.112), channel_id=1, source_target_pairs={{0,2},{1,3},{2,0},{3,1},{4,6},{5,7},{6,4},{7,5},{8,10},{9,11},{10,... | collective-permute-start | bytes 1179656 | tf_op jit(solution)/shard_map/ppermute | solution.py:669
  132.7 44.1 %collective-permute-start.26 = (bf16[16,48,384]{2,1,0:T(8,128)(2,1)}, bf16[16,48,384]{2,1,0:T(8,128)(2,1)S(1)}, u32[]{:S(2)}, u32[]{:S(2)}) collective-permute-start(bf16[16,48,384]{2,1,0:T(8,128)(2,1)} %constant_dynamic-update-slice_fusion.27.o0), channel_id=1, source_target_pairs={{0,1},{1,0},{2,3},{3,2},{4,5},{5,4},{6,7},{7,6},{8,9},{9,8},{10,11... | collective-permute-start | bytes 1769480 | tf_op jit(solution)/shard_map/ppermute | solution.py:669
  133.6 17.6 %collective-permute-start.13 = (bf16[16,48,640]{2,1,0:T(8,128)(2,1)}, bf16[16,48,640]{2,1,0:T(8,128)(2,1)}, u32[]{:S(2)}, u32[]{:S(2)}) collective-permute-start(bf16[16,48,640]{2,1,0:T(8,128)(2,1)} %constant_dynamic-update-slice_fusion.5.a0), channel_id=1, source_target_pairs={{0,1},{1,0},{2,3},{3,2},{4,5},{5,4},{6,7},{7,6},{8,9},{9,8},{10,11... | collective-permute-start | bytes 2949128 | tf_op jit(solution)/shard_map/ppermute | solution.py:669
  134.9 16.3 %collective-permute-start.19 = (bf16[16,48,512]{2,1,0:T(8,128)(2,1)}, bf16[16,48,512]{2,1,0:T(8,128)(2,1)S(1)}, u32[]{:S(2)}, u32[]{:S(2)}) collective-permute-start(bf16[16,48,512]{2,1,0:T(8,128)(2,1)} %constant_dynamic-update-slice_fusion.16.b0), channel_id=1, source_target_pairs={{0,1},{1,0},{2,3},{3,2},{4,5},{5,4},{6,7},{7,6},{8,9},{9,8},{10,11... | collective-permute-start | bytes 2359304 | tf_op jit(solution)/shard_map/ppermute | solution.py:669
  322.5 33.8 %collective-permute-start.73 = (f32[16,1024]{1,0:T(8,128)S(1)}, f32[16,1024]{1,0:T(8,128)S(1)}, u32[]{:S(2)}, u32[]{:S(2)}) collective-permute-start(f32[16,1024]{1,0:T(8,128)S(1)} %slice.447), channel_id=1, source_target_pairs={{0,1},{1,0},{2,3},{3,2},{4,5},{5,4},{6,7},{7,6},{8,9},{9,8},{10,11... | collective-permute-start | bytes 196616 | tf_op jit(solution)/shard_map/ppermute | solution.py:669
  327.2 31.2 %collective-permute-start.53 = (bf16[16,48,384]{2,1,0:T(8,128)(2,1)}, bf16[16,48,384]{2,1,0:T(8,128)(2,1)S(1)}, u32[]{:S(2)}, u32[]{:S(2)}) collective-permute-start(bf16[16,48,384]{2,1,0:T(8,128)(2,1)} %cols_grad_other.4), channel_id=1, source_target_pairs={{0,1},{1,0},{2,3},{3,2},{4,5},{5,4},{6,7},{7,6},{8,9},{9,8},{10,11... | collective-permute-start | bytes 1769480 | tf_op jit(solution)/shard_map/ppermute | solution.py:669
  333.2 39.1 %collective-permute-start.46 = (bf16[16,48,512]{2,1,0:T(8,128)(2,1)}, bf16[16,48,512]{2,1,0:T(8,128)(2,1)S(1)}, u32[]{:S(2)}, u32[]{:S(2)}) collective-permute-start(bf16[16,48,512]{2,1,0:T(8,128)(2,1)} %get-tuple-element.60), channel_id=1, source_target_pairs={{0,1},{1,0},{2,3},{3,2},{4,5},{5,4},{6,7},{7,6},{8,9},{9,8},{10,11... | collective-permute-start | bytes 2359304 | tf_op jit(solution)/shard_map/ppermute | solution.py:669
  352.2 62.8 %collective-permute-start.60 = (bf16[16,48,1536]{2,1,0:T(8,128)(2,1)}, bf16[16,48,1536]{2,1,0:T(8,128)(2,1)}, u32[]{:S(2)}, u32[]{:S(2)}) collective-permute-start(bf16[16,48,1536]{2,1,0:T(8,128)(2,1)} %cols_grad_other.5), channel_id=1, source_target_pairs={{0,1},{1,0},{2,3},{3,2},{4,5},{5,4},{6,7},{7,6},{8,9},{9,8},{10,11... | collective-permute-start | bytes 7077896 | tf_op jit(solution)/shard_map/ppermute | solution.py:669
  361.1 21.3 %collective-permute-start.40 = (bf16[16,48,640]{2,1,0:T(8,128)(2,1)S(1)}, bf16[16,48,640]{2,1,0:T(8,128)(2,1)S(1)}, u32[]{:S(2)}, u32[]{:S(2)}) collective-permute-start(bf16[16,48,640]{2,1,0:T(8,128)(2,1)S(1)} %copy-done.12), channel_id=1, source_target_pairs={{0,1},{1,0},{2,3},{3,2},{4,5},{5,4},{6,7},{7,6},{8,9},{9,8},{10,11... | collective-permute-start | bytes 2949128 | tf_op jit(solution)/shard_map/ppermute | solution.py:669
  363.1 27.3 %collective-permute-start.77 = (f32[1024]{0:T(1024)S(1)}, f32[1024]{0:T(1024)S(1)}, u32[]{:S(2)}, u32[]{:S(2)}) collective-permute-start(f32[1024]{0:T(1024)S(1)} %bitcast.205), channel_id=1, source_target_pairs={{0,8},{1,9},{2,10},{3,11},{4,12},{5,13},{6,14},{7,15},{8,0},{9,1},... | collective-permute-start | bytes 12296 | tf_op jit(solution)/shard_map/ppermute | solution.py:669
  390.4 36.7 %collective-permute-start.67 = (bf16[16,96,768]{2,1,0:T(8,128)(2,1)}, bf16[16,96,768]{2,1,0:T(8,128)(2,1)}, u32[]{:S(2)}, u32[]{:S(2)}) collective-permute-start(bf16[16,96,768]{2,1,0:T(8,128)(2,1)} %get-tuple-element.67), channel_id=1, source_target_pairs={{0,1},{1,0},{2,3},{3,2},{4,5},{5,4},{6,7},{7,6},{8,9},{9,8},{10,11... | collective-permute-start | bytes 7077896 | tf_op jit(solution)/shard_map/ppermute | solution.py:669
  417.5 25.9 %collective-permute-start.61 = (bf16[8,48,1536]{2,1,0:T(8,128)(2,1)S(1)}, bf16[8,48,1536]{2,1,0:T(8,128)(2,1)S(1)}, u32[]{:S(2)}, u32[]{:S(2)}) collective-permute-start(bf16[8,48,1536]{2,1,0:T(8,128)(2,1)S(1)} %slice.573), channel_id=1, source_target_pairs={{0,4},{1,5},{2,6},{3,7},{4,0},{5,1},{6,2},{7,3},{8,12},{9,13},{10,... | collective-permute-start | bytes 3538952 | tf_op jit(solution)/shard_map/ppermute | solution.py:669
  429.5 29.0 %collective-permute-start.68 = (bf16[8,96,768]{2,1,0:T(8,128)(2,1)S(1)}, bf16[8,96,768]{2,1,0:T(8,128)(2,1)S(1)}, u32[]{:S(2)}, u32[]{:S(2)}) collective-permute-start(bf16[8,96,768]{2,1,0:T(8,128)(2,1)S(1)} %slice.572), channel_id=1, source_target_pairs={{0,2},{1,3},{2,0},{3,1},{4,6},{5,7},{6,4},{7,5},{8,10},{9,11},{10,... | collective-permute-start | bytes 3538952 | tf_op jit(solution)/shard_map/ppermute | solution.py:669
  443.8 22.4 %collective-permute-start.62 = (bf16[4,48,1536]{2,1,0:T(8,128)(2,1)S(1)}, bf16[4,48,1536]{2,1,0:T(8,128)(2,1)S(1)}, u32[]{:S(2)}, u32[]{:S(2)}) collective-permute-start(bf16[4,48,1536]{2,1,0:T(8,128)(2,1)S(1)} %slice.575), channel_id=1, source_target_pairs={{0,2},{1,3},{2,0},{3,1},{4,6},{5,7},{6,4},{7,5},{8,10},{9,11},{10,... | collective-permute-start | bytes 1769480 | tf_op jit(solution)/shard_map/ppermute | solution.py:669
  471.2 17.9 %collective-permute-start.71 = (bf16[96,768]{1,0:T(8,128)(2,1)S(1)}, bf16[96,768]{1,0:T(8,128)(2,1)S(1)}, u32[]{:S(2)}, u32[]{:S(2)}) collective-permute-start(bf16[96,768]{1,0:T(8,128)(2,1)S(1)} %get-tuple-element.92), channel_id=1, source_target_pairs={{0,16},{1,17},{2,18},{3,19},{4,20},{5,21},{6,22},{7,23},{8,24},{9,... | collective-permute-start | bytes 442376 | tf_op jit(solution)/shard_map/ppermute | solution.py:669
  (63 other events, 552.2 us)
